TPU v7x, 32 devices: a whole 2x2x4 slice. The times are simulated.
32 devices in a mesh: seq: 4 (over x, core), rows: 8 (over z, y).
Axes of the slice: x: 2, y: 2, z: 4, core: 2. Of those that a mesh axis runs over, the one named last changes fastest.
Arguments:
- inputs: bfloat16 [16, 2048, 768], P('rows', 'seq'), may hold values from -6 to 6
- query_weight: bfloat16 [768, 768], replicated, may hold values from -0.21875 to 0.21875
- query_bias: bfloat16 [768], replicated, may hold values from -1.5 to 1.5
- key_weight: bfloat16 [768, 768], replicated, may hold values from -0.21875 to 0.21875
- value_weight: bfloat16 [768, 768], replicated, may hold values from -0.21875 to 0.21875
- value_bias: bfloat16 [768], replicated, may hold values from -1.5 to 1.5
- output_weight: bfloat16 [768, 768], replicated, may hold values from -1.5 to 1.5
- output_bias: bfloat16 [768], replicated, may hold values from -1.5 to 1.5
- first_gain: bfloat16 [768], replicated, may hold values from 0.5 to 1.5
- first_shift: bfloat16 [768], replicated, may hold values from -1 to 1
- inner_weight: bfloat16 [768, 3072], replicated, may hold values from -0.21875 to 0.21875
- inner_bias: bfloat16 [3072], replicated, may hold values from -1.5 to 1.5
- outer_weight: bfloat16 [3072, 768], replicated, may hold values from -0.109375 to 0.109375
- outer_bias: bfloat16 [768], replicated, may hold values from -1.5 to 1.5
- second_gain: bfloat16 [768], replicated, may hold values from 0.5 to 1.5
- second_shift: bfloat16 [768], replicated, may hold values from -1 to 1
- doc_tokens: int32 [16], P('rows'), may hold values from 512 to 2048, as said below
- random_blocks: int32 [16, 32, 3], P('rows'), may hold values from 2 to 31, as said below
- cotangent: bfloat16 [16, 2048, 768], P('rows', 'seq'), may hold values from -6 to 6
Outputs:
- outputs: bfloat16 [16, 2048, 768], P('rows', 'seq')
- input_gradient: bfloat16 [16, 2048, 768], P('rows', 'seq')
- query_weight_gradient: float32 [768, 768], replicated
- query_bias_gradient: float32 [768], replicated
- key_weight_gradient: float32 [768, 768], replicated
- value_weight_gradient: float32 [768, 768], replicated
- value_bias_gradient: float32 [768], replicated
- output_weight_gradient: float32 [768, 768], replicated
- output_bias_gradient: float32 [768], replicated
- first_gain_gradient: float32 [768], replicated
- first_shift_gradient: float32 [768], replicated
- inner_weight_gradient: float32 [768, 3072], replicated
- inner_bias_gradient: float32 [3072], replicated
- outer_weight_gradient: float32 [3072, 768], replicated
- outer_bias_gradient: float32 [768], replicated
- second_gain_gradient: float32 [768], replicated
- second_shift_gradient: float32 [768], replicated
Inputs may be any that keep to these rules, and one draw needn't show every extreme that they name: `doc_tokens`: in each aligned block of 2 rows one row, drawn from the seed, holds a document of more than 1536 tokens; one row of the batch, drawn from the seed, holds exactly 2048. `random_blocks`: for query block i of a row the 3 entries are distinct, and none of them is 0, 1, i - 1, i or i + 1.
All inputs are finite; a program needn't handle non-finite values.
Results may differ from a plain program's by a relative error of at most 0.015.
Values may be sent and summed in bfloat16 or wider, within the bound.
No kernel may reach another device: no remote copies, remote signals or barrier semaphores. Data moves between devices by JAX's collectives and lax.ppermute only.
A program may use at most 512 MiB of HBM per device.

v0:
```python
from functools import partial

import jax
import jax.numpy as jnp
from jax import lax
from jax.sharding import PartitionSpec as P

D = 768
HEADS = 12
HEAD = 64
BLOCK = 64


EPSILON = 1e-05
NEG_FILL = -1e30


def spread_2(block, axis, owner):
    block = jnp.where(lax.axis_index(axis) == owner, block, jnp.zeros_like(block))
    return lax.psum(block, axis)


def combined_all(array, axis, combine):
    everything = jax.tree.map(lambda part: lax.all_gather(part, axis), array)
    leading = jax.tree.map(lambda part: part[0], everything)

    def turn(k, so_far):
        return combine(so_far, jax.tree.map(lambda part: part[k], everything))

    return lax.fori_loop(1, lax.axis_size(axis), turn, leading)


def layer_norm(value, gain, shift):
    center = value - jnp.mean(value, -1, keepdims=True)
    spread = jnp.mean(center * center, -1, keepdims=True)
    return center * lax.rsqrt(spread + EPSILON) * gain + shift


def project(left, right):
    return jnp.einsum("rsd,de->rse", left, right, preferred_element_type=jnp.float32)


def project_back(left, right):
    return jnp.einsum("rse,de->rsd", left, right, preferred_element_type=jnp.float32)


def outer_sum(left, right):
    return jnp.einsum("rsd,rse->de", left, right, preferred_element_type=jnp.float32)


def column_sum(values):
    return jnp.sum(values.astype(jnp.float32), (0, 1))


def key_layout(block_ids, doc_tokens, random_blocks):
    row_count = random_blocks.shape[0]
    block_count = random_blocks.shape[1]
    before = block_ids - 1
    after_id = block_ids + 1
    fixed = jnp.stack([block_ids * 0, block_ids * 0 + 1, before, block_ids, after_id], -1)
    chosen = jnp.take(random_blocks, block_ids, axis=1)
    index = jnp.concatenate([jnp.broadcast_to(fixed, (row_count,) + fixed.shape), chosen], -1)
    always_on = block_ids >= 0
    allowed = jnp.stack(
        [always_on, always_on, before >= 2, always_on, after_id < block_count]
        + [always_on] * random_blocks.shape[2],
        -1,
    )
    index = jnp.clip(index, 0, block_count - 1)
    places = index[..., None] * BLOCK + jnp.arange(BLOCK, dtype=jnp.int32)
    valid = (places < doc_tokens[:, None, None, None]) & allowed[None, :, :, None]
    return (index, valid.reshape(row_count, block_ids.shape[0], -1))


def pick_keys(kv_full, index):
    row_count, full_len, both_width = kv_full.shape
    tiles = kv_full.reshape(row_count, full_len // BLOCK, BLOCK, both_width)
    chosen = jax.vmap(lambda tile_set, target: tile_set[target])(tiles, index)
    chosen = chosen.reshape(row_count, index.shape[1], -1, both_width)
    half = both_width // 2
    key_sel = chosen[..., :half].reshape(row_count, index.shape[1], -1, HEADS, HEAD)
    value_sel = chosen[..., half:].reshape(row_count, index.shape[1], -1, HEADS, HEAD)
    return (key_sel, value_sel)


def split_heads(blocks):
    return blocks.reshape(blocks.shape[:3] + (HEADS, HEAD))


def block_scores(query_blocks, key_sel, valid):
    score = jnp.einsum(
        "rgqhd,rgkhd->rghqk", split_heads(query_blocks), key_sel, preferred_element_type=jnp.float32
    ) * HEAD ** (-0.5)
    return jnp.where(valid[:, :, None, None, :], score, NEG_FILL)


def normal_forward(query_blocks, block_ids, kv_full, doc_tokens, random_blocks):
    index, valid = key_layout(block_ids, doc_tokens, random_blocks)
    key_sel, value_sel = pick_keys(kv_full, index)
    score = block_scores(query_blocks, key_sel, valid)
    row_max = jnp.max(score, -1, keepdims=True)
    expo = jnp.exp(score - row_max)
    row_sum = jnp.sum(expo, -1, keepdims=True)
    weight = (expo / row_sum).astype(jnp.bfloat16)
    context = jnp.einsum(
        "rghqk,rgkhd->rgqhd", weight, value_sel, preferred_element_type=jnp.float32
    )
    return (context.reshape(query_blocks.shape), row_max + jnp.log(row_sum))


def normal_backward(
    query_blocks, grad_blocks, block_ids, kv_full, doc_tokens, random_blocks, log_sum
):
    index, valid = key_layout(block_ids, doc_tokens, random_blocks)
    key_sel, value_sel = pick_keys(kv_full, index)
    score = block_scores(query_blocks, key_sel, valid)
    prob = jnp.exp(score - log_sum)
    split_grad = split_heads(grad_blocks)
    grad_prob = jnp.einsum(
        "rgqhd,rgkhd->rghqk", split_grad, value_sel, preferred_element_type=jnp.float32
    )
    delta = jnp.sum(prob * grad_prob, -1, keepdims=True)
    grad_score = (prob * (grad_prob - delta)).astype(jnp.bfloat16)
    scale = HEAD ** (-0.5)
    grad_query = (
        jnp.einsum("rghqk,rgkhd->rgqhd", grad_score, key_sel, preferred_element_type=jnp.float32)
        * scale
    )
    grad_key = (
        jnp.einsum(
            "rghqk,rgqhd->rgkhd",
            grad_score,
            split_heads(query_blocks),
            preferred_element_type=jnp.float32,
        )
        * scale
    )
    grad_value = jnp.einsum(
        "rghqk,rgqhd->rgkhd",
        prob.astype(jnp.bfloat16),
        split_grad,
        preferred_element_type=jnp.float32,
    )
    row_count, group = (index.shape[0], index.shape[1])
    pieces = jnp.concatenate(
        [grad_key.reshape(row_count, group, -1, D), grad_value.reshape(row_count, group, -1, D)], -1
    )
    pieces = pieces.reshape(row_count, -1, BLOCK, 2 * D)
    return (grad_query.reshape(query_blocks.shape), index.reshape(row_count, -1), pieces)


def add_blocks(accum, index, pieces):
    return jax.vmap(lambda tile_set, target, piece: tile_set.at[target].add(piece))(
        accum, index, pieces
    )


def combine_stats(earlier, later):
    joint = jnp.maximum(earlier[0], later[0])
    return (joint, earlier[1] * jnp.exp(earlier[0] - joint) + later[1] * jnp.exp(later[0] - joint))


def per_device(
    inputs,
    query_weight,
    query_bias,
    key_weight,
    value_weight,
    value_bias,
    output_weight,
    output_bias,
    first_gain,
    first_shift,
    inner_weight,
    inner_bias,
    outer_weight,
    outer_bias,
    second_gain,
    second_shift,
    doc_tokens,
    random_blocks,
    cotangent,
):
    row_count, seq_width = (inputs.shape[0], inputs.shape[1])
    seq_at = lax.axis_index("seq")
    per_dev = seq_width // BLOCK
    block_count = random_blocks.shape[1]
    full_len = block_count * BLOCK
    lead = 2 * BLOCK
    scale = HEAD ** (-0.5)
    query_local = (project(inputs, query_weight) + query_bias.astype(jnp.float32)).astype(
        jnp.bfloat16
    )
    key_local = project(inputs, key_weight).astype(jnp.bfloat16)
    value_local = (project(inputs, value_weight) + value_bias.astype(jnp.float32)).astype(
        jnp.bfloat16
    )
    kv_full = lax.all_gather(
        jnp.concatenate([key_local, value_local], -1), "seq", axis=1, tiled=True
    )
    own_ids = seq_at * per_dev + jnp.arange(per_dev, dtype=jnp.int32)
    query_blocks = query_local.reshape(row_count, per_dev, BLOCK, D)
    local_context, local_lse = normal_forward(
        query_blocks, own_ids, kv_full, doc_tokens, random_blocks
    )
    own_valid = (seq_at * seq_width + jnp.arange(seq_width, dtype=jnp.int32))[None, :] < doc_tokens[
        :, None
    ]
    score_mask = own_valid[:, None, None, :]
    key_heads = key_local.reshape(row_count, seq_width, HEADS, HEAD)
    value_heads = value_local.reshape(row_count, seq_width, HEADS, HEAD)
    lead_query = spread_2(query_local[:, :lead], "seq", 0)
    lead_heads = lead_query.reshape(row_count, lead, HEADS, HEAD)
    lead_score = (
        jnp.einsum("rqhd,rkhd->rhqk", lead_heads, key_heads, preferred_element_type=jnp.float32)
        * scale
    )
    lead_score = jnp.where(score_mask, lead_score, NEG_FILL)
    part_max = jnp.max(lead_score, -1, keepdims=True)
    part_sum = jnp.sum(
        jnp.where(score_mask, jnp.exp(lead_score - part_max), 0.0), -1, keepdims=True
    )
    lead_max, lead_sum = combined_all((part_max, part_sum), "seq", combine_stats)
    lead_prob = jnp.where(score_mask, jnp.exp(lead_score - (lead_max + jnp.log(lead_sum))), 0.0)
    lead_context = lax.psum(
        jnp.einsum(
            "rhqk,rkhd->rqhd",
            lead_prob.astype(jnp.bfloat16),
            value_heads,
            preferred_element_type=jnp.float32,
        ).astype(jnp.bfloat16),
        "seq",
    ).astype(jnp.float32)
    context = local_context.reshape(row_count, seq_width, D)
    context = jnp.where(
        seq_at == 0,
        jnp.concatenate([lead_context.reshape(row_count, lead, D), context[:, lead:]], 1),
        context,
    )
    context_low = context.astype(jnp.bfloat16)
    first_gain_f = first_gain.astype(jnp.float32)
    first_shift_f = first_shift.astype(jnp.float32)
    second_gain_f = second_gain.astype(jnp.float32)
    second_shift_f = second_shift.astype(jnp.float32)
    resid = (
        inputs.astype(jnp.float32)
        + project(context_low, output_weight)
        + output_bias.astype(jnp.float32)
    )
    first = layer_norm(resid, first_gain_f, first_shift_f)
    first_low = first.astype(jnp.bfloat16)
    inner = project(first_low, inner_weight) + inner_bias.astype(jnp.float32)
    active_low = jax.nn.gelu(inner, approximate=True).astype(jnp.bfloat16)
    second = first + project(active_low, outer_weight) + outer_bias.astype(jnp.float32)
    result = layer_norm(second, second_gain_f, second_shift_f)
    second_pull = jax.vjp(layer_norm, second, second_gain_f, second_shift_f)[1]
    d_second, second_gain_grad, second_shift_grad = second_pull(cotangent.astype(jnp.float32))
    d_outer = d_second.astype(jnp.bfloat16)
    gelu_pull = jax.vjp(partial(jax.nn.gelu, approximate=True), inner)[1]
    d_inner = gelu_pull(project_back(d_outer, outer_weight))[0].astype(jnp.bfloat16)
    d_first = d_second + project_back(d_inner, inner_weight)
    first_pull = jax.vjp(layer_norm, resid, first_gain_f, first_shift_f)[1]
    d_resid, first_gain_grad, first_shift_grad = first_pull(d_first)
    d_attended = d_resid.astype(jnp.bfloat16)
    d_context = project_back(d_attended, output_weight).astype(jnp.bfloat16)
    keep = (own_ids >= 2).astype(jnp.bfloat16)
    grad_blocks = d_context.reshape(row_count, per_dev, BLOCK, D) * keep[None, :, None, None]
    lead_grad = spread_2(d_context[:, :lead], "seq", 0)
    lead_grad_heads = lead_grad.reshape(row_count, lead, HEADS, HEAD)
    lead_grad_prob = jnp.einsum(
        "rqhd,rkhd->rhqk", lead_grad_heads, value_heads, preferred_element_type=jnp.float32
    )
    lead_delta = lax.psum(jnp.sum(lead_prob * lead_grad_prob, -1, keepdims=True), "seq")
    lead_grad_score = (lead_prob * (lead_grad_prob - lead_delta)).astype(jnp.bfloat16)
    lead_grad_query = lax.psum(
        (
            jnp.einsum(
                "rhqk,rkhd->rqhd", lead_grad_score, key_heads, preferred_element_type=jnp.float32
            )
            * scale
        ).astype(jnp.bfloat16),
        "seq",
    ).astype(jnp.float32)
    lead_grad_key = (
        jnp.einsum(
            "rhqk,rqhd->rkhd", lead_grad_score, lead_heads, preferred_element_type=jnp.float32
        )
        * scale
    )
    lead_grad_value = jnp.einsum(
        "rhqk,rqhd->rkhd",
        lead_prob.astype(jnp.bfloat16),
        lead_grad_heads,
        preferred_element_type=jnp.float32,
    )
    lead_kv = jnp.concatenate(
        [
            lead_grad_key.reshape(row_count, seq_width, D),
            lead_grad_value.reshape(row_count, seq_width, D),
        ],
        -1,
    )
    empty = jnp.zeros((row_count, block_count, BLOCK, 2 * D), jnp.float32)
    local_dq, index, pieces = normal_backward(
        query_blocks, grad_blocks, own_ids, kv_full, doc_tokens, random_blocks, local_lse
    )
    own_kv = lax.psum_scatter(
        add_blocks(empty, index, pieces).reshape(row_count, full_len, 2 * D).astype(jnp.bfloat16),
        "seq",
        scatter_dimension=1,
        tiled=True,
    ).astype(jnp.float32)
    own_kv = own_kv + lead_kv
    lead_pad = jnp.pad(
        lead_grad_query.reshape(row_count, lead, D), ((0, 0), (0, seq_width - lead), (0, 0))
    )
    d_query = local_dq.reshape(row_count, seq_width, D) + jnp.where(seq_at == 0, lead_pad, 0.0)
    d_query_low = d_query.astype(jnp.bfloat16)
    d_key_low = own_kv[..., :D].astype(jnp.bfloat16)
    d_value_low = own_kv[..., D:].astype(jnp.bfloat16)
    d_input = (
        d_resid
        + project_back(d_query_low, query_weight)
        + project_back(d_key_low, key_weight)
        + project_back(d_value_low, value_weight)
    )
    summed = lax.psum(
        (
            outer_sum(inputs, d_query_low),
            column_sum(d_query_low),
            outer_sum(inputs, d_key_low),
            outer_sum(inputs, d_value_low),
            column_sum(d_value_low),
            outer_sum(context_low, d_attended),
            column_sum(d_attended),
            first_gain_grad,
            first_shift_grad,
            outer_sum(first_low, d_inner),
            column_sum(d_inner),
            outer_sum(active_low, d_outer),
            column_sum(d_outer),
            second_gain_grad,
            second_shift_grad,
        ),
        ("seq", "rows"),
    )
    return (result.astype(jnp.bfloat16), d_input.astype(jnp.bfloat16)) + tuple(summed)


def solution(mesh):
    in_specs = (
        P("rows", "seq", None),
        P(),
        P(),
        P(),
        P(),
        P(),
        P(),
        P(),
        P(),
        P(),
        P(),
        P(),
        P(),
        P(),
        P(),
        P(),
        P("rows"),
        P("rows", None, None),
        P("rows", "seq", None),
    )
    out_specs = (
        P("rows", "seq", None),
        P("rows", "seq", None),
        P(),
        P(),
        P(),
        P(),
        P(),
        P(),
        P(),
        P(),
        P(),
        P(),
        P(),
        P(),
        P(),
        P(),
        P(),
    )
    return jax.shard_map(
        per_device, mesh=mesh, in_specs=in_specs, out_specs=out_specs, check_vma=False
    )
```

profile of v0, /device:TPU:0, one launch (start us, length us, event | category | flops | bytes accessed | tf_op | source)
XLA Modules:
  0.0 1414.0 jit_solution(2700706302214810185)
XLA Ops:
  25.8 5.9 reshape.373
  36.1 6.7 copy.166
  42.9 6.0 all-reduce.9.cloned.1.call-done
  51.1 5.2 all-gather
  58.2 5.2 all-gather.1
  63.9 5.9 convolution_convert_fusion.2
  69.9 63.4 %all-gather.4.cloned.1.call-done = bf16[2,2048,1536]{2,1,0:T(8,128)(2,1)} async-done(((bf16[2,512,1536]{2,1,0:T(8,128)(2,1)}), bf16[2,2048,1536]{2,1,0:T(8,128)(2,1)}) %all-gather.4.cloned.1.call-update) | async-done | bytes 12582928 | tf_op jit(solution)/shard_map/all_gather | solution.py:198
  133.2 16.0 %gather_fusion = bf16[128,64,1536]{2,1,0:T(8,128)(2,1)} fusion(bf16[2,32,64,1536]{3,2,1,0:T(8,128)(2,1)} %bitcast.188, s32[128]{0:T(128)S(1)} %reshape.339), kind=kCustom, calls=%fused_computation.1 | custom fusion | bytes 50332672 | tf_op jit(solution)/shard_map/vmap()/gather | solution.py:78
  149.2 17.4 %fusion.85 = (bf16[2,8,512,768]{3,2,1,0:T(8,128)(2,1)}, bf16[2,8,512,768]{3,2,1,0:T(8,128)(2,1)}) fusion(bf16[2,8,512,1536]{3,2,1,0:T(8,128)(2,1)} %bitcast.183), kind=kLoop, calls=%fused_computation.170 | loop fusion | bytes 50331648 | tf_op jit(solution)/shard_map/slice | solution.py:81
  166.7 16.7 %copy.197 = bf16[2,8,512,768]{2,3,1,0:T(8,128)(2,1)} copy(bf16[2,8,512,768]{3,2,1,0:T(8,128)(2,1)} %get-tuple-element.279) | data formatting | bytes 25165824
  183.4 16.7 %copy.196 = bf16[2,8,512,768]{2,3,1,0:T(8,128)(2,1)} copy(bf16[2,8,512,768]{3,2,1,0:T(8,128)(2,1)} %get-tuple-element.280) | data formatting | bytes 25165824
  200.0 14.4 %fusion.15 = (f32[2,8,12,64]{3,2,1,0:T(8,128)S(1)}, f32[2,8,12,64,512]{4,3,2,1,0:T(8,128)}) fusion(pred[2,8,512]{2,1,0:T(8,128)(4,1)S(1)} %fusion.63, bf16[2,8,64,12,64]{2,4,3,1,0:T(8,128)(2,1)} %copy.166, bf16[2,8,512,12,64]{2,4,3,1,0:T(8,128)(2,1)} %bitcast.181), kind=kOutput, calls=%fused_computation.32 | convolution fusion | flops 824168448 | bytes 39378944 | tf_op jit(solution)/shard_map/rgqhd,rgkhd->rghqk/dot_general | solution.py:91
  214.5 11.6 fusion.2
  226.1 15.2 %fusion.39 = bf16[2,8,64,12,64]{2,4,3,1,0:T(8,128)(2,1)S(1)} fusion(bf16[2,8,512,12,64]{2,4,3,1,0:T(8,128)(2,1)} %bitcast.186, f32[2,8,12,64]{3,2,1,0:T(8,128)S(1)} %fusion.2, f32[2,8,12,64]{3,2,1,0:T(8,128)S(1)} %get-tuple-element.288, f32[2,8,12,64,512]{4,3,2,1,0:T(8,128)} %get-tuple-element.289, pred[2,8,512]{2,1,0:T(8,128)(4,1)S(1)} %fusion.63), kind=kOutput, calls=%fused_computation.87 | convolution fusion | flops 836763648 | bytes 39428096 | tf_op jit(solution)/shard_map/rghqk,rgkhd->rgqhd/dot_general | solution.py:105
  241.4 4.5 copy.159
  245.9 4.9 reshape_reshape.12
  258.3 8.1 fusion.27
  266.4 10.6 fusion.87
  284.4 16.1 %convert_reduce_fusion = (f32[3072]{0:T(1024)}, bf16[2,512,3072]{2,1,0:T(8,128)(2,1)S(1)}) fusion(f32[2,512,3072]{2,1,0:T(8,128)} %fusion.27, f32[3072]{0:T(1024)S(1)} %convert_element_type.152, bf16[2,512,768]{2,1,0:T(8,128)(2,1)S(1)} %get-tuple-element.272, bf16[3072,768]{1,0:T(8,128)(2,1)} %param.35), kind=kOutput, calls=%fused_computation.28 | convolution fusion | flops 4904186880 | bytes 25190400 | tf_op jit(solution)/shard_map/rse,de->rsd/dot_general | solution.py:44
  300.5 11.5 multiply_reduce_fusion.2
  324.1 25.3 %multiply_reduce_fusion = (f32[2,8,12,64]{3,2,1,0:T(8,128)S(1)}, f32[2,8,12,64,512]{4,3,2,1,0:T(8,128)}) fusion(f32[2,8,12,64]{3,2,1,0:T(8,128)S(1)} %log_add_fusion, f32[2,8,12,64,512]{4,3,2,1,0:T(8,128)} %get-tuple-element.289, pred[2,8,512]{2,1,0:T(8,128)(4,1)S(1)} %fusion.63, bf16[2,8,512,12,64]{2,4,3,1,0:T(8,128)(2,1)} %bitcast.187, ...), kind=kOutput, calls=%fused_computation.11 | convolution fusion | flops 836751360 | bytes 64593920 | tf_op jit(solution)/shard_map/rgqhd,rgkhd->rghqk/dot_general | solution.py:119
  349.4 19.7 %fusion.16 = f32[2,8,512,12,64]{2,4,3,1,0:T(8,128)} fusion(f32[2,8,12,64]{3,2,1,0:T(8,128)S(1)} %log_add_fusion, f32[2,8,12,64,512]{4,3,2,1,0:T(8,128)} %get-tuple-element.289, pred[2,8,512]{2,1,0:T(8,128)(4,1)S(1)} %fusion.63, bf16[2,8,64,12,64]{2,1,4,3,0:T(8,128)(2,1)S(1)} %broadcast_multiply_fusion), kind=kOutput, calls=%fused_computation.33 | convolution fusion | flops 830472192 | bytes 51961856 | tf_op jit(solution)/shard_map/rghqk,rgqhd->rgkhd/dot_general | solution.py:138
  370.0 22.6 %multiply_convert_fusion = bf16[2,8,12,64,512]{4,3,2,1,0:T(8,128)(2,1)} fusion(f32[2,8,12,64,512]{4,3,2,1,0:T(8,128)} %get-tuple-element.300, f32[2,8,12,64]{3,2,1,0:T(8,128)S(1)} %get-tuple-element.299, f32[2,8,12,64]{3,2,1,0:T(8,128)S(1)} %log_add_fusion, f32[2,8,12,64,512]{4,3,2,1,0:T(8,128)} %get-tuple-element.289, pred[2,8,512]{2,1,0:T(8,128)(4,1)S(1)} %fusion.63), kind=kLoop, calls=%fused_computation.10 | loop fusion | flops 37748736 | bytes 63021056 | tf_op jit(solution)/shard_map/convert_element_type | solution.py:123
  392.7 16.3 %multiply_bitcast_fusion = f32[2,8,512,12,64]{2,4,3,1,0:T(8,128)} fusion(bf16[2,8,64,12,64]{2,4,3,1,0:T(8,128)(2,1)S(1)} %copy-done.4, bf16[2,8,12,64,512]{4,3,2,1,0:T(8,128)(2,1)} %multiply_convert_fusion), kind=kOutput, calls=%fused_computation.9 | convolution fusion | flops 811597824 | bytes 39321600 | tf_op jit(solution)/shard_map/rghqk,rgqhd->rgkhd/dot_general | solution.py:130
  409.0 27.5 %copy.169 = f32[2,8,512,12,64]{2,1,4,3,0:T(8,128)} copy(f32[2,8,512,12,64]{2,4,3,1,0:T(8,128)} %fusion.16) | data formatting | bytes 50331648 | tf_op jit(solution)/shard_map/rghqk,rgqhd->rgkhd/transpose | solution.py:138
  436.6 16.7 %copy.167 = f32[2,8,512,12,64]{2,1,4,3,0:T(8,128)} copy(f32[2,8,512,12,64]{2,4,3,1,0:T(8,128)S(1)} %copy-done.2) | data formatting | bytes 50331648 | tf_op jit(solution)/shard_map/mul | solution.py:130
  453.3 36.4 %concatenate.40 = f32[2,64,64,768]{2,1,3,0:T(8,128)} reshape(f32[2,8,512,12,64]{2,1,4,3,0:T(8,128)} %copy.167) | data formatting | bytes 50331648 | tf_op jit(solution)/shard_map/concatenate | solution.py:145
  489.7 36.7 %concatenate.41 = f32[2,64,64,768]{2,1,3,0:T(8,128)} reshape(f32[2,8,512,12,64]{2,1,4,3,0:T(8,128)} %copy.169) | data formatting | bytes 50331648 | tf_op jit(solution)/shard_map/concatenate | solution.py:145
  526.4 7.8 multiply_reduce_fusion.1
  534.3 10.1 psum.143
  544.4 5.7 multiply_convert_fusion.2
  553.7 67.3 %pad_maximum_fusion = f32[2,64,64,1536]{2,1,3,0:T(8,128)} fusion(f32[2,64,64,768]{2,1,3,0:T(8,128)} %concatenate.41, f32[2,64,64,768]{2,1,3,0:T(8,128)} %concatenate.40), kind=kLoop, calls=%fused_computation.8 | loop fusion | flops 12582912 | bytes 100663296 | tf_op jit(solution)/shard_map/concatenate | solution.py:145
  621.1 72.1 %copy.170 = f32[2,64,64,1536]{3,2,1,0:T(8,128)} copy(f32[2,64,64,1536]{2,1,3,0:T(8,128)} %pad_maximum_fusion) | data formatting | bytes 100663296 | tf_op jit(solution)/shard_map/concatenate | solution.py:145
  693.2 11.5 broadcast_in_dim.126
  704.7 118.0 %scatter_fusion = f32[2,32,64,1536]{3,2,1,0:T(8,128)} fusion(f32[2,32,64,1536]{3,2,1,0:T(8,128)} %broadcast_in_dim.126, s32[128]{0:T(128)S(1)} %copy-done.16, f32[128,64,1536]{2,1,0:T(8,128)} %bitcast.180), kind=kCustom, calls=%fused_computation.2 | custom fusion | flops 12582912 | bytes 150995968 | tf_op jit(solution)/shard_map/vmap()/scatter-add | solution.py:153
  822.7 13.4 convert_element_type.170
  836.2 11.4 multiply_bitcast_fusion.1
  847.7 8.9 copy.163
  856.6 6.5 reshape_reshape.13
  867.5 10.9 convolution_bitcast_fusion.1
  878.4 13.2 convolution_bitcast_fusion
  911.7 25.6 %reduce-scatter.2.cloned.1.call-done = bf16[2,512,1536]{2,1,0:T(8,128)(2,1)} async-done(((bf16[2,2048,1536]{2,1,0:T(8,128)(2,1)}), bf16[2,512,1536]{2,1,0:T(8,128)(2,1)}) %reduce-scatter.2.cloned.1.call-update) | async-done | bytes 3145744 | tf_op jit(solution)/shard_map/reduce_scatter | solution.py:307
  937.4 4.7 fusion.19
  948.0 4.6 fusion.56
  952.9 42.6 %all-reduce.1 = (f32[768]{0:T(1024)}, f32[768]{0:T(1024)}, f32[768]{0:T(1024)}, f32[768]{0:T(1024)}, f32[768]{0:T(1024)}, /*index=5*/f32[3072]{0:T(1024)}, f32[768]{0:T(1024)}, f32[768]{0:T(1024)}, f32[768]{0:T(1024)}) all-reduce(f32[768]{0:T(1024)S(1)} %get-tuple-element.275, ...), channel_id=1, replica_groups=mesh['seq'=4,'rows'=8] {'seq','rows'}, use_global_device_ids=true, to_apply=%region_25.27 | all-reduce | flops 9216 | bytes 73728 | tf_op jit(solution)/shard_map/psum | solution.py:327
  999.5 4.9 add_convert_fusion
  1004.5 379.7 %all-reduce.17.cloned.1.call-done = (f32[768,768]{0,1:T(8,128)}, f32[768,768]{0,1:T(8,128)}, f32[768,768]{0,1:T(8,128)}, f32[768,768]{1,0:T(8,128)}, f32[768,3072]{1,0:T(8,128)}, /*index=5*/f32[3072,768]{1,0:T(8,128)}) async-done(((f32[768,768]{0,1:T(8,128)}, f32[768,768]{0,1:T(8,128)}, f32[768,768]{0,1:T(8,128)}, f32[768,768]{1,0:T(8,128)}, f32[768,3072]{1,0:T(8,128)}, /*index=5*/f32[3072,768]{1,0:T(8,128)}), ...) | async-done | bytes 28311568 | tf_op jit(solution)/shard_map/psum | solution.py:327
  1393.9 9.3 copy.229
  (296 shorter events, 106.7 us)
Async XLA Ops:
  7.2 246.7 %copy-start = (bf16[768,768]{1,0:T(8,128)(2,1)S(1)}, bf16[768,768]{1,0:T(8,128)(2,1)}, u32[]{:S(2)}) copy-start(bf16[768,768]{1,0:T(8,128)(2,1)} %param.29) | copy-start | bytes 3538948
  7.2 41.7 %all-reduce.9.cloned.1.call-start = ((), (), s32[]{:S(2)}) async-start(), calls=%async_computation.1 | async-start | bytes 786432 | tf_op jit(solution)/shard_map/psum | solution.py:20
  13.4 119.8 %all-gather.4.cloned.1.call-start = ((), (), s32[]{:S(2)}) async-start(), calls=%async_computation.3 | async-start | bytes 15728640 | tf_op jit(solution)/shard_map/all_gather | solution.py:198
  20.8 231.2 %all-reduce.11.cloned.1.call-start = ((), (), s32[]{:S(2)}) async-start(), calls=%async_computation.2 | async-start | bytes 786432 | tf_op jit(solution)/shard_map/psum | solution.py:225
  22.6 26.3 %copy-start.10 = (bf16[2,512,768]{1,2,0:T(8,128)(2,1)}, bf16[2,512,768]{1,2,0:T(8,128)(2,1)S(1)}, u32[]{:S(2)}) copy-start(bf16[2,512,768]{1,2,0:T(8,128)(2,1)S(1)} %copy.140) | copy-start | bytes 4718596
  25.8 6.6 copy-start.69
  25.8 6.6 copy-start.70
  25.8 6.6 copy-start.71
  25.8 7.6 copy-start.60
  25.8 7.6 copy-start.63
  31.8 280.2 %copy-start.34 = (f32[768]{0:T(1024)}, f32[768]{0:T(1024)S(1)}, u32[]{:S(2)}) copy-start(f32[768]{0:T(1024)S(1)} %convert_element_type.149) | copy-start | bytes 9220
  32.4 234.0 %copy-start.37 = (f32[768]{0:T(1024)}, f32[768]{0:T(1024)S(1)}, u32[]{:S(2)}) copy-start(f32[768]{0:T(1024)S(1)} %convert_element_type.150) | copy-start | bytes 9220
  33.4 250.9 %copy-start.57 = (f32[3072]{0:T(1024)}, f32[3072]{0:T(1024)S(1)}, u32[]{:S(2)}) copy-start(f32[3072]{0:T(1024)S(1)} %convert_element_type.152) | copy-start | bytes 36868
  36.1 6.7 copy-start.64
  42.8 21.0 %copy-start.44 = (pred[2,512]{1,0:T(4,128)(4,1)}, pred[2,512]{1,0:T(4,128)(4,1)S(1)}, u32[]{:S(2)}) copy-start(pred[2,512]{1,0:T(4,128)(4,1)S(1)} %broadcast_compare_fusion.2) | copy-start | bytes 3076
  51.1 7.1 copy-start.3
  56.3 7.5 copy-start.20
  69.8 456.6 %all-reduce.13.cloned.1.call-start = ((), (), s32[]{:S(2)}) async-start(), calls=%async_computation.4 | async-start | bytes 786432 | tf_op jit(solution)/shard_map/psum | solution.py:20
  254.0 12.4 slice-start.5
  257.7 54.4 %copy-start.8 = (f32[2,512,768]{2,1,0:T(8,128)}, f32[2,512,768]{2,1,0:T(8,128)S(1)}, u32[]{:S(2)}) copy-start(f32[2,512,768]{2,1,0:T(8,128)S(1)} %get-tuple-element.293) | copy-start | bytes 9437188
  257.7 54.4 %copy-start.42 = (f32[2,512]{1,0:T(2,128)}, f32[2,512]{1,0:T(2,128)S(1)}, u32[]{:S(2)}) copy-start(f32[2,512]{1,0:T(2,128)S(1)} %broadcast_multiply_fusion.3) | copy-start | bytes 12292
  258.2 53.8 %copy-start.49 = (f32[2,512]{1,0:T(2,128)}, f32[2,512]{1,0:T(2,128)S(1)}, u32[]{:S(2)}) copy-start(f32[2,512]{1,0:T(2,128)S(1)} %fusion.70) | copy-start | bytes 12292
  258.2 8.1 slice-start.6
  266.4 10.7 copy-start.12
  266.4 10.7 copy-start.51
  284.4 16.1 %copy-start.29 = (bf16[2,512,768]{2,1,0:T(8,128)(2,1)}, bf16[2,512,768]{2,1,0:T(8,128)(2,1)S(1)}, u32[]{:S(2)}) copy-start(bf16[2,512,768]{2,1,0:T(8,128)(2,1)S(1)} %get-tuple-element.272) | copy-start | bytes 4718596
  300.5 11.5 copy-start.19
  370.0 536.5 %all-reduce.15.cloned.1.call-start = ((), (), s32[]{:S(2)}) async-start(), calls=%async_computation.5 | async-start | bytes 786432 | tf_op jit(solution)/shard_map/psum | solution.py:275
  370.0 22.7 %copy-start.4 = (bf16[2,8,64,12,64]{2,4,3,1,0:T(8,128)(2,1)S(1)}, bf16[2,8,64,12,64]{2,4,3,1,0:T(8,128)(2,1)}, u32[]{:S(2)}) copy-start(bf16[2,8,64,12,64]{2,4,3,1,0:T(8,128)(2,1)} %copy.166) | copy-start | bytes 4718596
  409.0 27.5 %copy-start.2 = (f32[2,8,512,12,64]{2,4,3,1,0:T(8,128)S(1)}, f32[2,8,512,12,64]{2,4,3,1,0:T(8,128)}, u32[]{:S(2)}) copy-start(f32[2,8,512,12,64]{2,4,3,1,0:T(8,128)} %multiply_bitcast_fusion) | copy-start | bytes 75497472
  489.7 36.7 %copy-start.21 = (bf16[2,512,768]{1,2,0:T(8,128)(2,1)S(1)}, bf16[2,512,768]{1,2,0:T(8,128)(2,1)}, u32[]{:S(2)}) copy-start(bf16[2,512,768]{1,2,0:T(8,128)(2,1)} %copy.138) | copy-start | bytes 4718596
  489.7 36.7 %copy-start.40 = (f32[2,12,128]{2,1,0:T(8,128)S(1)}, f32[2,12,128]{2,1,0:T(8,128)}, u32[]{:S(2)}) copy-start(f32[2,12,128]{2,1,0:T(8,128)} %copy-done.39) | copy-start | bytes 36868
  489.7 36.7 %copy-start.45 = (pred[2,512]{1,0:T(4,128)(4,1)S(1)}, pred[2,512]{1,0:T(4,128)(4,1)}, u32[]{:S(2)}) copy-start(pred[2,512]{1,0:T(4,128)(4,1)} %copy-done.44) | copy-start | bytes 3076
  544.4 7.4 copy-start.11
  553.7 383.7 %reduce-scatter.2.cloned.1.call-start = ((), (), s32[]{:S(2)}) async-start(), calls=%async_computation.6 | async-start | bytes 15728640 | tf_op jit(solution)/shard_map/reduce_scatter | solution.py:307
  693.2 11.5 copy-start.16
  836.2 548.0 %all-reduce.17.cloned.1.call-start = ((), (), s32[]{:S(2)}) async-start(), calls=%async_computation.7 | async-start | bytes 56623104 | tf_op jit(solution)/shard_map/psum | solution.py:327
  867.5 10.9 copy-start.30
  867.5 10.9 copy-start.58
  867.5 24.1 %slice-start = ((s8[6291456]{0:T(1024)(128)(4,1)}), s8[4194304]{0:T(1024)(128)(4,1)S(1)}, s32[]{:S(2)}) async-start(s8[6291456]{0:T(1024)(128)(4,1)} %bitcast.184), calls=%async_computation.8 | async-start | bytes 8388608
  878.4 13.2 slice-start.1
  878.4 13.2 copy-start.36
  878.4 13.2 copy-start.41
  878.4 13.2 copy-start.46
  948.0 50.9 %copy-start.33 = (bf16[768,768]{1,0:T(8,128)(2,1)S(1)}, bf16[768,768]{1,0:T(8,128)(2,1)}, u32[]{:S(2)}) copy-start(bf16[768,768]{1,0:T(8,128)(2,1)} %param.27) | copy-start | bytes 3538948
  1392.5 10.7 slice-start.2
  1393.9 9.3 slice-start.3
  1393.9 9.3 slice-start.4
  (44 other events, 174.5 us)
Sparse Core Ops, SparseCore 0:
  13.5 35.3 all-reduce.8
  51.1 82.0 all-gather.3
  136.3 32.6 all-reduce.10
  370.1 32.6 all-reduce.12
  553.8 33.1 all-reduce.14
  836.3 101.0 reduce-scatter.1
  948.0 436.1 all-reduce.16
where the time goes:
time: 1430 us; the launch traced here: 1410 us
  waiting for transfers between devices  475 us (33%)
  local copies, waits for them, and re-layouts  357 us (25%)
  other arithmetic  267 us (19%)
  matrix products  236 us (17%)
  blocking collectives  63.2 us (4%)
  between operations  15.5 us (1%)
    psum x1, waiting for transfers between devices, per_device(): lax.psum((outer_sum(inputs, d_query_low), column_sum(d_query_low), outer_...  380 us
    concatenate x3, local copies, waits for them, and re-layouts, normal_backward(): jnp.concatenate([grad_key.reshape(row_count, group, -1, D), grad_value.re...  145 us
    scatter-add x2, other arithmetic, add_blocks(): tile_set.at[target].add(piece)  118 us
    concatenate x1, other arithmetic, normal_backward(): jnp.concatenate([grad_key.reshape(row_count, group, -1, D), grad_value.re...  67.3 us
    all_gather x1, waiting for transfers between devices, per_device(): lax.all_gather(jnp.concatenate([key_local, value_local], -1), 'seq', axis...  63.4 us
    unnamed x179, local copies, waits for them, and re-layouts  62.4 us
    psum x1, blocking collectives, per_device(): lax.psum((outer_sum(inputs, d_query_low), column_sum(d_query_low), outer_...  42.6 us
    dot_general x6, matrix products, project_back(): jnp.einsum('rse,de->rsd', left, right, preferred_element_type=jnp.float32)  41.9 us
  transfers between devices with their start and end apart: 7, of which 4 were waited for; matrix products, arithmetic and copies ran while one was open for 48% of the time, Pallas kernels for 0%

commit v1 on v0

v1 whole, which is shorter than its diff:
```python
import functools
from functools import partial

import jax
import jax.numpy as jnp
from jax import lax
from jax.experimental import pallas as pl
from jax.experimental.pallas import tpu as pltpu
from jax.sharding import PartitionSpec as P

D = 768
HEADS = 12
HEAD = 64
BLOCK = 64
SETS = 8
CHIPS_Z = 4

EPSILON = 1e-05
NEG_FILL = -1e30

NT = (((1,), (1,)), ((), ()))
NN = (((1,), (0,)), ((), ()))
TN = (((0,), (0,)), ((), ()))


def dot(left, right, dims):
    return lax.dot_general(left, right, dims, preferred_element_type=jnp.float32)


def head_groups(heads):
    groups, at = [], 0
    while at < heads:
        n = 2 if heads - at >= 2 else 1
        groups.append((at, n))
        at += n
    return groups


def spread_heads(block, diag, n):
    if n == 1:
        return block
    w = n * HEAD
    return jnp.concatenate([block] * n, 0) * diag[:w, :w]


def fold_heads(full, diag, n):
    if n == 1:
        return full
    w = n * HEAD
    kept = full * diag[:w, :w]
    out = kept[:HEAD]
    for h in range(1, n):
        out = out + kept[h * HEAD : (h + 1) * HEAD]
    return out


def rows_of(slot):
    return pl.ds(pl.multiple_of(slot * BLOCK, BLOCK), BLOCK)


def gather_rows(ref, slots, lanes):
    return jnp.concatenate([ref[rows_of(s), lanes] for s in slots], 0)


def attend_kernel(
    heads,
    nb,
    key_at_ref,
    bias_at_ref,
    query_at_ref,
    q_ref,
    k_ref,
    v_ref,
    bias_ref,
    diag_ref,
    o_ref,
    lse_ref,
    top_ref,
    sum_ref,
    acc_ref,
):
    groups = head_groups(heads)
    scale = jnp.bfloat16(HEAD**-0.5)

    def local(t, carry):
        ks = [key_at_ref[t, b] for b in range(SETS)]
        bs = [bias_at_ref[t, b] for b in range(SETS)]
        qs = query_at_ref[t]
        bias = gather_rows(bias_ref, bs, slice(None))
        diag = diag_ref[...]
        diag_f = diag.astype(jnp.float32)
        for at, n in groups:
            w = n * HEAD
            lanes = slice(at * HEAD, at * HEAD + w)
            query = spread_heads(q_ref[rows_of(qs), lanes] * scale, diag, n)
            score = dot(gather_rows(k_ref, ks, lanes), query, NT) + bias[:, :w]
            top = jnp.max(score, 0, keepdims=True)
            prob = jnp.exp(score - top)
            total = jnp.sum(prob, 0, keepdims=True)
            prob = (prob * (1.0 / total)).astype(jnp.bfloat16)
            out = fold_heads(dot(prob, gather_rows(v_ref, ks, lanes), TN), diag_f, n)
            o_ref[rows_of(qs), lanes] = out.astype(jnp.bfloat16)
            lse_ref[qs, :, lanes] = top + jnp.log(total)
        return carry

    lax.fori_loop(0, nb - 2, local, 0)

    chunks = nb // SETS

    def lead(b, carry):
        qs = query_at_ref[nb - 2 + b * chunks]
        top_ref[...] = jnp.full_like(top_ref, NEG_FILL)
        sum_ref[...] = jnp.zeros_like(sum_ref)
        acc_ref[...] = jnp.zeros_like(acc_ref)
        diag = diag_ref[...]
        diag_f = diag.astype(jnp.float32)

        def chunk(c, carry):
            keys = pl.ds(pl.multiple_of(c * (SETS * BLOCK), SETS * BLOCK), SETS * BLOCK)
            bias = bias_ref[keys, :]
            for at, n in groups:
                w = n * HEAD
                lanes = slice(at * HEAD, at * HEAD + w)
                query = spread_heads(q_ref[rows_of(qs), lanes] * scale, diag, n)
                score = dot(k_ref[keys, lanes], query, NT) + bias[:, :w]
                was = top_ref[:, lanes]
                top = jnp.maximum(was, jnp.max(score, 0, keepdims=True))
                prob = jnp.exp(score - top)
                keep = jnp.exp(was - top)
                top_ref[:, lanes] = top
                sum_ref[:, lanes] = sum_ref[:, lanes] * keep + jnp.sum(prob, 0, keepdims=True)
                part = dot(v_ref[keys, lanes], prob.astype(jnp.bfloat16), TN)
                acc_ref[lanes, :w] = acc_ref[lanes, :w] * keep + part
            return carry

        lax.fori_loop(0, chunks, chunk, 0)
        for at, n in groups:
            w = n * HEAD
            lanes = slice(at * HEAD, at * HEAD + w)
            total = sum_ref[:, lanes]
            full = (acc_ref[lanes, :w] * (1.0 / total)).T
            o_ref[rows_of(qs), lanes] = fold_heads(full, diag_f, n).astype(jnp.bfloat16)
            lse_ref[qs, :, lanes] = top_ref[:, lanes] + jnp.log(total)
        return carry

    lax.fori_loop(0, 2, lead, 0)


def attend_back_kernel(
    heads,
    nb,
    tasks,
    key_at_ref,
    bias_at_ref,
    query_at_ref,
    q_ref,
    k_ref,
    v_ref,
    g_ref,
    bias_ref,
    diag_ref,
    lse_ref,
    delta_ref,
    dq_ref,
    dk_ref,
    dv_ref,
    dq_acc,
    dk_acc,
    dv_acc,
):
    groups = head_groups(heads)
    dq_acc[...] = jnp.zeros_like(dq_acc)
    dk_acc[...] = jnp.zeros_like(dk_acc)
    dv_acc[...] = jnp.zeros_like(dv_acc)
    scale = HEAD**-0.5

    def task(t, carry):
        ks = [key_at_ref[t, b] for b in range(SETS)]
        bs = [bias_at_ref[t, b] for b in range(SETS)]
        qs = query_at_ref[t]
        bias = gather_rows(bias_ref, bs, slice(None))
        diag = diag_ref[...]
        diag_f = diag.astype(jnp.float32)
        for at, n in groups:
            w = n * HEAD
            lanes = slice(at * HEAD, at * HEAD + w)
            query = spread_heads(q_ref[rows_of(qs), lanes] * jnp.bfloat16(scale), diag, n)
            grad = spread_heads(g_ref[rows_of(qs), lanes], diag, n)
            keys = gather_rows(k_ref, ks, lanes)
            values = gather_rows(v_ref, ks, lanes)
            score = dot(keys, query, NT) + bias[:, :w]
            prob = jnp.exp(score - lse_ref[qs, :, lanes])
            d_prob = dot(values, grad, NT)
            d_score = (prob * (d_prob - delta_ref[qs, :, lanes])).astype(jnp.bfloat16)
            d_value = dot(prob.astype(jnp.bfloat16), grad, NN)
            d_key = dot(d_score, query, NN)
            before = [(dk_acc[rows_of(a), lanes], dv_acc[rows_of(a), lanes]) for a in bs]
            for i, a in enumerate(bs):
                part = slice(i * BLOCK, (i + 1) * BLOCK)
                dk_acc[rows_of(a), lanes] = before[i][0] + d_key[part]
                dv_acc[rows_of(a), lanes] = before[i][1] + d_value[part]
            d_query = fold_heads(dot(d_score, keys, TN), diag_f, n)
            dq_acc[rows_of(qs), lanes] += d_query * scale
        return carry

    lax.fori_loop(0, tasks, task, 0)
    dq_ref[...] = dq_acc[...].astype(jnp.bfloat16)
    dk_ref[...] = dk_acc[: nb * BLOCK].astype(jnp.bfloat16)
    dv_ref[...] = dv_acc[: nb * BLOCK].astype(jnp.bfloat16)


VMEM = pl.BlockSpec(memory_space=pltpu.VMEM)
SMEM = pl.BlockSpec(memory_space=pltpu.SMEM)


def diagonal_mask():
    head = jnp.arange(2 * HEAD) // HEAD
    return (head[:, None] == head[None, :]).astype(jnp.bfloat16)


def attend(q, k, v, tables, heads, nb):
    key_at, bias_at, query_at, bias = tables
    width = heads * HEAD
    return pl.pallas_call(
        partial(attend_kernel, heads, nb),
        out_shape=(
            jax.ShapeDtypeStruct((nb * BLOCK, width), jnp.bfloat16),
            jax.ShapeDtypeStruct((nb, 1, width), jnp.float32),
        ),
        in_specs=[SMEM] * 3 + [VMEM] * 5,
        out_specs=(VMEM, VMEM),
        scratch_shapes=[
            pltpu.VMEM((1, width), jnp.float32),
            pltpu.VMEM((1, width), jnp.float32),
            pltpu.VMEM((width, 2 * HEAD), jnp.float32),
        ],
        compiler_params=pltpu.CompilerParams(vmem_limit_bytes=48 << 20),
        cost_estimate=pl.CostEstimate(
            flops=40_000_000_000, bytes_accessed=8 << 20, transcendentals=0
        ),
        name="attend",
    )(key_at, bias_at, query_at, q, k, v, bias, diagonal_mask())


def attend_back(q, k, v, grad, tables, lse, delta, heads, nb):
    key_at, bias_at, query_at, bias = tables
    width = heads * HEAD
    out = jax.ShapeDtypeStruct((nb * BLOCK, width), jnp.bfloat16)
    return pl.pallas_call(
        partial(attend_back_kernel, heads, nb, key_at.shape[0]),
        out_shape=(out, out, out),
        in_specs=[SMEM] * 3 + [VMEM] * 8,
        out_specs=(VMEM, VMEM, VMEM),
        scratch_shapes=[
            pltpu.VMEM((nb * BLOCK, width), jnp.float32),
            pltpu.VMEM(((nb + 1) * BLOCK, width), jnp.float32),
            pltpu.VMEM(((nb + 1) * BLOCK, width), jnp.float32),
        ],
        compiler_params=pltpu.CompilerParams(vmem_limit_bytes=52 << 20),
        cost_estimate=pl.CostEstimate(
            flops=45_000_000_000, bytes_accessed=10 << 20, transcendentals=0
        ),
        name="attend_back",
    )(key_at, bias_at, query_at, q, k, v, grad, bias, diagonal_mask(), lse, delta)


def block_tables(block_of_slot, doc, random_blocks):
    nb = random_blocks.shape[0]
    every = jnp.arange(nb, dtype=jnp.int32)
    slot_of_block = jnp.sum(
        jnp.where(block_of_slot[None, :] == every[:, None], every[None, :], 0), 1
    )
    ids = every[2:]
    before, after = ids - 1, ids + 1
    always_on = ids >= 0
    index = jnp.concatenate(
        [jnp.stack([ids * 0, ids * 0 + 1, before, ids, after], -1), random_blocks[2:]], -1
    )
    allowed = jnp.stack(
        [always_on, always_on, before >= 2, always_on, after < nb] + [always_on] * 3, -1
    )
    index = jnp.clip(index, 0, nb - 1)
    slots = jnp.sum(jnp.where(index[..., None] == block_of_slot, every, 0), -1)
    chunks = nb // SETS
    lead = jnp.tile(every.reshape(chunks, SETS), (2, 1))
    key_at = jnp.concatenate([slots, lead], 0)
    bias_at = jnp.concatenate([jnp.where(allowed, slots, nb), lead], 0)
    query_at = jnp.concatenate([slot_of_block[2:], jnp.repeat(slot_of_block[:2], chunks)])
    places = block_of_slot[:, None] * BLOCK + jnp.arange(BLOCK, dtype=jnp.int32)
    bias = jnp.where(places < doc, 0.0, NEG_FILL).astype(jnp.float32).reshape(-1)
    bias = jnp.concatenate([bias, jnp.full((BLOCK,), NEG_FILL, jnp.float32)])
    bias = jnp.broadcast_to(bias[:, None], (bias.shape[0], 2 * HEAD))
    return key_at, bias_at, query_at, bias


class Ring:
    def __init__(self, axis, size, at, perm):
        self.axis, self.size, self.at, self.perm = axis, size, at, perm

    def send(self, value, by):
        return lax.ppermute(value, self.axis, self.perm(by))

    def scatter_sum(self, value):
        part = value.shape[0] // self.size

        def cut(i):
            return lax.dynamic_slice_in_dim(value, lax.rem(i, self.size) * part, part, 0)

        if self.size == 1:
            return value
        total = cut(self.at).astype(jnp.float32)
        for by in range(1, self.size):
            total = total + self.send(cut(self.at + by), by).astype(jnp.float32)
        return total.astype(value.dtype)

    def gather(self, value):
        if self.size == 1:
            return value
        part = value.shape[0]
        if self.size == 2:
            other = self.send(value, 1)
            first = jnp.where(self.at == 0, value, other)
            second = jnp.where(self.at == 0, other, value)
            return jnp.concatenate([first, second], 0)
        out = jnp.zeros((self.size * part,) + value.shape[1:], value.dtype)
        out = lax.dynamic_update_slice_in_dim(out, value, self.at * part, 0)
        for by in range(1, self.size):
            came = lax.rem(self.at + self.size - by, self.size)
            out = lax.dynamic_update_slice_in_dim(out, self.send(value, by), came * part, 0)
        return out


def make_rings(seq, rows):
    half = seq // 2
    deep = CHIPS_Z if rows % CHIPS_Z == 0 else 1
    wide = rows // deep
    s, r = lax.axis_index("seq"), lax.axis_index("rows")
    near = Ring(
        "seq",
        half,
        lax.rem(s, half),
        lambda by: [(i, i // half * half + (i + by) % half) for i in range(seq)],
    )
    far = Ring("seq", 2, s // half, lambda by: [(i, (i + half) % seq) for i in range(seq)])
    y = Ring(
        "rows",
        wide,
        lax.rem(r, wide),
        lambda by: [(i, i // wide * wide + (i + by) % wide) for i in range(rows)],
    )
    z = Ring("rows", deep, r // wide, lambda by: [(i, (i + by * wide) % rows) for i in range(rows)])
    return near, far, y, z


def summed(value, order):
    for ring in order:
        value = ring.scatter_sum(value)
    for ring in reversed(order):
        value = ring.gather(value)
    return value


def layer_norm(value, gain, shift):
    center = value - jnp.mean(value, -1, keepdims=True)
    spread = jnp.mean(center * center, -1, keepdims=True)
    return center * lax.rsqrt(spread + EPSILON) * gain + shift


def column_sum(values):
    return jnp.sum(values.astype(jnp.float32), 0)


def per_device(
    seq,
    rows,
    inputs,
    query_weight,
    query_bias,
    key_weight,
    value_weight,
    value_bias,
    output_weight,
    output_bias,
    first_gain,
    first_shift,
    inner_weight,
    inner_bias,
    outer_weight,
    outer_bias,
    second_gain,
    second_shift,
    doc_tokens,
    random_blocks,
    cotangent,
):
    low, full = jnp.bfloat16, jnp.float32
    near, far, y, z = make_rings(seq, rows)
    half = seq // 2
    width = inputs.shape[1]
    nb = random_blocks.shape[1]
    heads = HEADS // half
    cols = heads * HEAD
    mine, at = far.at, near.at

    def to_rows(array):
        own = lax.dynamic_index_in_dim(array, mine, 0, False)
        return own, far.send(lax.dynamic_index_in_dim(array, 1 - mine, 0, False), 1)

    def from_rows(value):
        own, other = value[:width], far.send(value[width:], 1)
        return jnp.where(mine == 0, jnp.stack([own, other]), jnp.stack([other, own]))

    x_pair = jnp.concatenate(to_rows(inputs), 0)
    tokens = x_pair.shape[0]
    x_all = jnp.concatenate([x_pair] + [near.send(x_pair, half - k) for k in range(1, half)], 0)
    cot = jnp.concatenate(to_rows(cotangent), 0)

    shards = []
    for k in range(half):
        own = mine * half + lax.rem(at + k, half)
        shards += [own, lax.rem(own + half, seq)]
    per_shard = width // BLOCK
    block_of_slot = (
        jnp.stack(shards)[:, None] * per_shard + jnp.arange(per_shard, dtype=jnp.int32)
    ).reshape(-1).astype(jnp.int32)
    doc = lax.dynamic_index_in_dim(doc_tokens, mine, 0, False)
    chosen = lax.dynamic_index_in_dim(random_blocks, mine, 0, False)
    tables = block_tables(block_of_slot, doc, chosen)

    def my_cols(weight):
        return lax.dynamic_slice_in_dim(weight, at * cols, cols, weight.ndim - 1)

    wq, wk, wv = my_cols(query_weight), my_cols(key_weight), my_cols(value_weight)
    query = (dot(x_all, wq, NN) + my_cols(query_bias).astype(full)).astype(low)
    key = dot(x_all, wk, NN).astype(low)
    value = (dot(x_all, wv, NN) + my_cols(value_bias).astype(full)).astype(low)

    heads_context, lse = attend(query, key, value, tables, heads, nb)
    context = jnp.concatenate(
        [heads_context[:tokens]]
        + [near.send(heads_context[k * tokens : (k + 1) * tokens], k) for k in range(1, half)],
        1,
    )
    wo = jnp.concatenate(
        [
            lax.dynamic_slice_in_dim(
                output_weight, lax.rem(at + half - k, half) * cols, cols, 0
            )
            for k in range(half)
        ],
        0,
    )
    first_gain_f, first_shift_f = first_gain.astype(full), first_shift.astype(full)
    second_gain_f, second_shift_f = second_gain.astype(full), second_shift.astype(full)
    resid = x_pair.astype(full) + dot(context, wo, NN) + output_bias.astype(full)
    first = layer_norm(resid, first_gain_f, first_shift_f)
    first_low = first.astype(low)
    inner = dot(first_low, inner_weight, NN) + inner_bias.astype(full)
    active = jax.nn.gelu(inner, approximate=True).astype(low)
    second = first + dot(active, outer_weight, NN) + outer_bias.astype(full)
    result = layer_norm(second, second_gain_f, second_shift_f).astype(low)
    result = from_rows(result)

    second_pull = jax.vjp(layer_norm, second, second_gain_f, second_shift_f)[1]
    d_second, second_gain_grad, second_shift_grad = second_pull(cot.astype(full))
    d_outer = d_second.astype(low)
    outer_grad = dot(active, d_outer, TN).astype(low)
    gelu_pull = jax.vjp(partial(jax.nn.gelu, approximate=True), inner)[1]
    d_inner = gelu_pull(dot(d_outer, outer_weight, NT))[0].astype(low)
    inner_grad = dot(first_low, d_inner, TN).astype(low)
    d_first = d_second + dot(d_inner, inner_weight, NT)
    first_pull = jax.vjp(layer_norm, resid, first_gain_f, first_shift_f)[1]
    d_resid, first_gain_grad, first_shift_grad = first_pull(d_first)
    d_attended = d_resid.astype(low)
    out_grad = dot(context, d_attended, TN)
    out_grad = jnp.concatenate(
        [
            lax.dynamic_slice_in_dim(out_grad, lax.rem(at + half - k, half) * cols, cols, 0)
            for k in range(half)
        ],
        0,
    )
    d_context = dot(d_attended, wo, NT).astype(low)
    heads_grad = jnp.concatenate(
        [d_context[:, :cols]]
        + [near.send(d_context[:, k * cols : (k + 1) * cols], half - k) for k in range(1, half)],
        0,
    )
    delta = jnp.sum(
        (heads_grad.astype(full) * heads_context.astype(full)).reshape(nb, BLOCK, heads, HEAD), -1
    )
    delta = delta.transpose(0, 2, 1).reshape(nb, 1, cols)
    d_query, d_key, d_value = attend_back(
        query, key, value, heads_grad, tables, lse, delta, heads, nb
    )
    d_part = (dot(d_query, wq, NT) + dot(d_key, wk, NT) + dot(d_value, wv, NT)).astype(low)
    d_input = d_resid + d_part[:tokens].astype(full)
    for k in range(1, half):
        d_input = d_input + near.send(d_part[k * tokens : (k + 1) * tokens], k).astype(full)
    d_input = from_rows(d_input.astype(low))

    vectors = (
        column_sum(d_attended),
        first_gain_grad,
        first_shift_grad,
        column_sum(d_inner),
        column_sum(d_outer),
        second_gain_grad,
        second_shift_grad,
    )
    packed = jnp.concatenate(vectors).reshape(-1, D)
    packed = jnp.pad(packed, ((0, 128 - packed.shape[0]), (0, 0)))
    out_grad = jnp.concatenate([out_grad, packed], 0).astype(low)
    outer_grad = summed(outer_grad, [near, far, y, z]).astype(full)
    inner_grad = summed(inner_grad, [near, y, z, far]).astype(full)
    out_grad = summed(out_grad, [near, z, far, y]).astype(full)

    def with_bias(weight_grad, bias_grad):
        extra = jnp.pad(bias_grad[None, :], ((0, 31), (0, 0)))
        return jnp.concatenate([weight_grad, extra], 0).astype(low)

    def heads_summed(value, order):
        value = summed(value, order)
        parts = near.gather(value[None])
        return jnp.concatenate([parts[k] for k in range(half)], 1).astype(full)

    query_grad = heads_summed(
        with_bias(dot(x_all, d_query, TN), column_sum(d_query)), [far, y, z]
    )
    key_grad = heads_summed(dot(x_all, d_key, TN).astype(low), [y, z, far])
    value_grad = heads_summed(
        with_bias(dot(x_all, d_value, TN), column_sum(d_value)), [z, far, y]
    )
    at_768 = out_grad[D:]
    return (
        result,
        d_input,
        query_grad[:D],
        query_grad[D],
        key_grad,
        value_grad[:D],
        value_grad[D],
        out_grad[:D],
        at_768[0],
        at_768[1],
        at_768[2],
        inner_grad,
        at_768[3:7].reshape(-1),
        outer_grad,
        at_768[7],
        at_768[8],
        at_768[9],
    )


def solution(mesh):
    tokens = P("rows", "seq", None)
    in_specs = (tokens,) + (P(),) * 15 + (P("rows"), P("rows", None, None), tokens)
    out_specs = (tokens, tokens) + (P(),) * 15
    return jax.shard_map(
        partial(per_device, mesh.shape["seq"], mesh.shape["rows"]),
        mesh=mesh,
        in_specs=in_specs,
        out_specs=out_specs,
        check_vma=False,
    )
```

time: 1430 us -> 669 us (0.47)
  local copies, waits for them, and re-layouts: 357 us -> 55.9 us
  waiting for transfers between devices: 475 us -> 225 us
  other arithmetic: 267 us -> 78 us
  matrix products: 236 us -> 111 us
  starting transfers between devices: 0.29 us -> 104 us
  Pallas kernels: 0 us -> 84.8 us
  blocking collectives: 63.2 us -> 0 us
    psum x5 -> x0, waiting for transfers between devices: 386 us -> none  [the longest x1 380 us: per_device(): lax.psum((outer_sum(inputs, d_query_low), column_sum(d_query_low), outer_...]
    ppermute x0 -> x77, waiting for transfers between devices: none -> 225 us  [send(): return lax.ppermute(value, self.axis, self.perm(by))]
    concatenate x4 -> x5, local copies, waits for them, and re-layouts: 145 us -> 0.38 us  [the longest x1 0.35 us: per_device(): packed = jnp.concatenate(vectors).reshape(-1, D)]
    dot_general x30 -> x18, matrix products: 236 us -> 111 us  [dot(): lax.dot_general(left, right, dims, preferred_element_type=jnp.float32)]
    scatter-add x2 -> x0, other arithmetic: 118 us -> none  [add_blocks(): tile_set.at[target].add(piece)]
    ppermute x0 -> x77, starting transfers between devices: none -> 104 us  [send(): return lax.ppermute(value, self.axis, self.perm(by))]
    pallas_call x0 -> x2, Pallas kernels: none -> 84.8 us  [the longest x1 44.6 us: attend_back(): pl.pallas_call(partial(attend_back_kernel, heads, nb, key_at.shape[0]), o...]
    all_gather x1 -> x0, waiting for transfers between devices: 63.4 us -> none  [per_device(): lax.all_gather(jnp.concatenate([key_local, value_local], -1), 'seq', axis...]
  transfers between devices with their start and end apart: 7 -> 77, of which waited for: 4 -> 32; matrix products, arithmetic and copies ran while one was open for 48% -> 25% of each run, Pallas kernels for 0% -> 13%
where the time goes in v1:
time: 669 us; the launch traced here: 661 us
  waiting for transfers between devices  225 us (34%)
  matrix products  111 us (17%)
  starting transfers between devices  104 us (16%)
  Pallas kernels  84.8 us (13%)
  other arithmetic  78 us (12%)
  local copies, waits for them, and re-layouts  55.9 us (8%)
    ppermute x77, waiting for transfers between devices, send(): return lax.ppermute(value, self.axis, self.perm(by))  225 us
    dot_general x18, matrix products, dot(): lax.dot_general(left, right, dims, preferred_element_type=jnp.float32)  111 us
    ppermute x77, starting transfers between devices, send(): return lax.ppermute(value, self.axis, self.perm(by))  104 us
    pallas_call x1, Pallas kernels, attend_back(): pl.pallas_call(partial(attend_back_kernel, heads, nb, key_at.shape[0]), o...  44.6 us
    pallas_call x1, Pallas kernels, attend(): pl.pallas_call(partial(attend_kernel, heads, nb), out_shape=(jax.ShapeDty...  40.2 us
  transfers between devices with their start and end apart: 77, of which 32 were waited for; matrix products, arithmetic and copies ran while one was open for 25% of the time, Pallas kernels for 13%

profile of v1, /device:TPU:0, one launch (start us, length us, event | category | flops | bytes accessed | tf_op | source)
XLA Modules:
  0.0 661.2 jit_solution(10301429684816274437)
XLA Ops:
  0.7 3.7 constant_dynamic-slice_fusion.39
  12.5 30.7 %collective-permute-done = bf16[512,768]{0,1:T(8,128)(2,1)} collective-permute-done((bf16[512,768]{0,1:T(8,128)(2,1)S(1)}, bf16[512,768]{0,1:T(8,128)(2,1)}, u32[]{:S(2)}, u32[]{:S(2)}) %collective-permute-start) | collective-permute-done | bytes 786464 | tf_op jit(solution)/shard_map/ppermute | solution.py:301
  49.4 3.6 convolution_convert_fusion.2.k_ref
  53.0 5.2 add_convert_fusion.5.v_ref
  58.2 3.4 add_convert_fusion.6.q_ref
  62.0 40.2 %attend.1 = (bf16[2048,384]{1,0:T(8,128)(2,1)S(1)}, f32[32,1,384]{2,1,0:T(1,128)S(1)}) custom-call(s32[38,8]{1,0:T(8,128)S(1)} %get-tuple-element.199.key_at_ref, s32[38,8]{1,0:T(8,128)S(1)} %get-tuple-element.198.bias_at_ref, s32[38]{0:T(128)S(1)} %pad_add_fusion.2.query_at_ref, bf16[2048,384]{1,0:T(8,128)(2,1)S(1)} %add_convert_fusion.6.q_ref, ...), custom_call_target="tpu_custom_call" | custom-call | flops 40000000000 | bytes 8388608 | tf_op jit(solution)/shard_map/attend/pallas_call | solution.py:224
  109.7 3.8 fusion.50
  113.9 8.7 %fusion.41 = f32[1024,3072]{1,0:T(8,128)} fusion(bf16[768,3072]{1,0:T(8,128)(2,1)S(1)} %bitcast.90, f32[1024,768]{0,1:T(8,128)S(1)} %get-tuple-element.207, f32[768]{0:T(1024)S(1)} %convert_element_type.371, f32[768]{0:T(1024)S(1)} %convert_element_type.370, f32[1024]{0:T(1024)S(1)} %fusion.35, f32[1024]{0:T(1024)S(1)} %broadcast_multiply_fusion.1), kind=kOutput, calls=%fused_computation.263 | convolution fusion | flops 4835770368 | bytes 20461568 | tf_op jit(solution)/shard_map/dot_general | solution.py:27
  122.7 11.5 %fusion.51 = (f32[1024]{0:T(1024)S(1)}, f32[1024,768]{0,1:T(8,128)S(1)}) fusion(f32[768]{0:T(1024)S(1)} %convert_element_type.375, bf16[3072,768]{1,0:T(8,128)(2,1)} %param.31, f32[1024,3072]{1,0:T(8,128)} %fusion.41, f32[3072]{0:T(1024)S(1)} %convert_element_type.373, f32[768]{0:T(1024)S(1)} %convert_element_type.371, f32[768]{0:T(1024)S(1)} %convert_element_type.370, ...), kind=kOutput, calls=%fused_computation.272 | convolution fusion | flops 4868799488 | bytes 23626752 | tf_op jit(solution)/shard_map/dot_general | solution.py:27
  141.8 13.0 %convolution_convert_fusion = bf16[3072,768]{1,0:T(8,128)(2,1)} fusion(bf16[1024,768]{0,1:T(8,128)(2,1)S(1)} %get-tuple-element.113, f32[1024,3072]{1,0:T(8,128)} %fusion.41, f32[3072]{0:T(1024)S(1)} %convert_element_type.373), kind=kOutput, calls=%fused_computation.11 | convolution fusion | flops 4865654784 | bytes 18886656 | tf_op jit(solution)/shard_map/dot_general | solution.py:27
  154.9 16.9 %fusion.52 = (bf16[3072]{0:T(1024)(128)(2,1)S(1)}, bf16[1024,3072]{1,0:T(8,128)(2,1)}) fusion(f32[1024,3072]{1,0:T(8,128)} %fusion.41, f32[3072]{0:T(1024)S(1)} %convert_element_type.373, bf16[1024,768]{0,1:T(8,128)(2,1)S(1)} %get-tuple-element.113, bf16[3072,768]{1,0:T(8,128)(2,1)} %param.31), kind=kOutput, calls=%fused_computation.273 | convolution fusion | flops 4901041152 | bytes 25184256 | tf_op jit(solution)/shard_map/dot_general | solution.py:27
  174.8 10.3 %convolution_convert_fusion.1 = bf16[768,3072]{1,0:T(8,128)(2,1)} fusion(bf16[1024,3072]{1,0:T(8,128)(2,1)} %get-tuple-element.212, f32[1024,768]{0,1:T(8,128)S(1)} %get-tuple-element.207, f32[768]{0:T(1024)S(1)} %convert_element_type.371, f32[768]{0:T(1024)S(1)} %convert_element_type.370, f32[1024]{0:T(1024)S(1)} %fusion.35, ...), kind=kOutput, calls=%fused_computation.12 | convolution fusion | flops 4838129664 | bytes 14170112 | tf_op jit(solution)/shard_map/dot_general | solution.py:27
  185.1 7.8 %multiply_reduce_fusion = (bf16[768]{0:T(1024)(128)(2,1)S(1)}, f32[1024]{0:T(1024)S(1)}, bf16[768]{0:T(1024)(128)(2,1)S(1)}, f32[1024,768]{0,1:T(8,128)S(1)}) fusion(f32[1024,768]{0,1:T(8,128)S(1)} %get-tuple-element.207, f32[1024]{0:T(1024)S(1)} %fusion.35, f32[1024]{0:T(1024)S(1)} %broadcast_multiply_fusion.1, f32[768]{0:T(1024)S(1)} %convert_element_type.370, ...), kind=kOutput, calls=%fused_computation.26 | convolution fusion | flops 4847563776 | bytes 22057984 | tf_op jit(solution)/shard_map/dot_general | solution.py:27
  219.7 3.7 copy.103
  223.3 6.1 reshape.297
  229.5 3.6 reduce_sum.191
  235.9 44.6 %attend_back.1 = (bf16[2048,384]{1,0:T(8,128)(2,1)}, bf16[2048,384]{1,0:T(8,128)(2,1)}, bf16[2048,384]{1,0:T(8,128)(2,1)}) custom-call(s32[38,8]{1,0:T(8,128)S(1)} %get-tuple-element.199.key_at_ref, s32[38,8]{1,0:T(8,128)S(1)} %get-tuple-element.198.bias_at_ref, s32[38]{0:T(128)S(1)} %pad_add_fusion.2.query_at_ref, bf16[2048,384]{1,0:T(8,128)(2,1)} %copy-done.4, ...), custom_call_target="tpu_custom_call" | custom-call | flops 44999999488 | bytes 10485760 | tf_op jit(solution)/shard_map/attend_back/pallas_call | solution.py:249
  282.2 6.0 fusion.25
  293.6 3.5 fusion.22
  297.1 3.5 convolution_convert_fusion.5
  302.3 3.4 convolution_convert_fusion.4
  305.8 3.5 convolution_convert_fusion.6
  323.8 6.3 collective-permute-done.31
  341.5 5.3 collective-permute-start.20
  346.9 3.9 collective-permute-start.21
  363.6 3.7 collective-permute-start.12
  369.5 4.0 collective-permute-start.51
  387.8 3.8 collective-permute-done.13
  397.3 3.3 collective-permute-start.28
  400.7 3.4 add_convert_fusion.2
  407.6 28.6 %collective-permute-done.16 = bf16[200,384]{1,0:T(8,128)(2,1)S(1)} collective-permute-done((bf16[200,384]{1,0:T(8,128)(2,1)S(1)}, bf16[200,384]{1,0:T(8,128)(2,1)S(1)}, u32[]{:S(2)}, u32[]{:S(2)}) %collective-permute-start.16) | collective-permute-done | bytes 153632 | tf_op jit(solution)/shard_map/ppermute | solution.py:301
  445.7 5.0 collective-permute-done.55
  450.7 4.8 collective-permute-done.57
  455.5 13.9 %collective-permute-done.56 = bf16[48,3072]{1,0:T(8,128)(2,1)S(1)} collective-permute-done((bf16[48,3072]{1,0:T(8,128)(2,1)S(1)}, bf16[48,3072]{1,0:T(8,128)(2,1)S(1)}, u32[]{:S(2)}, u32[]{:S(2)}) %collective-permute-start.56) | collective-permute-done | bytes 294944 | tf_op jit(solution)/shard_map/ppermute | solution.py:301
  470.8 17.3 %collective-permute-done.58 = bf16[24,3072]{1,0:T(8,128)(2,1)S(1)} collective-permute-done((bf16[24,3072]{1,0:T(8,128)(2,1)S(1)}, bf16[24,3072]{1,0:T(8,128)(2,1)S(1)}, u32[]{:S(2)}, u32[]{:S(2)}) %collective-permute-start.58) | collective-permute-done | bytes 147488 | tf_op jit(solution)/shard_map/ppermute | solution.py:301
  494.1 8.9 %collective-permute-done.67 = bf16[384,768]{1,0:T(8,128)(2,1)S(1)} collective-permute-done((bf16[384,768]{1,0:T(8,128)(2,1)S(1)}, bf16[384,768]{1,0:T(8,128)(2,1)S(1)}, u32[]{:S(2)}, u32[]{:S(2)}) %collective-permute-start.67) | collective-permute-done | bytes 589856 | tf_op jit(solution)/shard_map/ppermute | solution.py:301
  504.0 8.3 %collective-permute-start.70 = (bf16[96,768]{1,0:T(8,128)(2,1)S(1)}, bf16[96,768]{1,0:T(8,128)(2,1)S(1)}, u32[]{:S(2)}, u32[]{:S(2)}) collective-permute-start(bf16[96,768]{1,0:T(8,128)(2,1)S(1)} %get-tuple-element.166), channel_id=1, source_target_pairs={{0,6},{1,7},{2,0},{3,1},{4,2},{5,3},{6,4},{7,5},{8,14},{9,15},{10,... | collective-permute-start | bytes 442376 | tf_op jit(solution)/shard_map/ppermute | solution.py:301
  512.9 4.2 collective-permute-done.68
  517.6 6.1 collective-permute-done.69
  525.9 13.0 %collective-permute-done.61 = bf16[48,3072]{1,0:T(8,128)(2,1)S(1)} collective-permute-done((bf16[48,3072]{1,0:T(8,128)(2,1)S(1)}, bf16[48,3072]{1,0:T(8,128)(2,1)S(1)}, u32[]{:S(2)}, u32[]{:S(2)}) %collective-permute-start.61) | collective-permute-done | bytes 294944 | tf_op jit(solution)/shard_map/ppermute | solution.py:301
  538.9 11.6 %collective-permute-start.71 = (bf16[96,768]{1,0:T(8,128)(2,1)S(1)}, bf16[96,768]{1,0:T(8,128)(2,1)S(1)}, u32[]{:S(2)}, u32[]{:S(2)}) collective-permute-start(bf16[96,768]{1,0:T(8,128)(2,1)S(1)} %get-tuple-element.109), channel_id=1, source_target_pairs={{0,2},{1,3},{2,4},{3,5},{4,6},{5,7},{6,0},{7,1},{8,10},{9,11},{10,... | collective-permute-start | bytes 442376 | tf_op jit(solution)/shard_map/ppermute | solution.py:301
  550.5 6.0 collective-permute-done.71
  567.7 30.0 %collective-permute-done.74 = bf16[384,768]{1,0:T(8,128)(2,1)S(1)} collective-permute-done((bf16[384,768]{1,0:T(8,128)(2,1)S(1)}, bf16[384,768]{1,0:T(8,128)(2,1)S(1)}, u32[]{:S(2)}, u32[]{:S(2)}) %collective-permute-start.74) | collective-permute-done | bytes 589856 | tf_op jit(solution)/shard_map/ppermute | solution.py:301
  602.5 3.4 slice.143
  611.5 16.8 %collective-permute-done.75 = bf16[768,768]{1,0:T(8,128)(2,1)} collective-permute-done((bf16[768,768]{1,0:T(8,128)(2,1)}, bf16[768,768]{1,0:T(8,128)(2,1)}, u32[]{:S(2)}, u32[]{:S(2)}) %collective-permute-start.75) | collective-permute-done | bytes 1179680 | tf_op jit(solution)/shard_map/ppermute | solution.py:301
  638.4 3.4 collective-permute-done.7
  648.6 5.0 maximum_convert_fusion
  656.2 4.5 maximum_convert_fusion.1
  (472 shorter events, 197.0 us)
Async XLA Ops:
  5.5 102.8 %collective-permute-start.4 = (bf16[512,768]{0,1:T(8,128)(2,1)}, bf16[512,768]{0,1:T(8,128)(2,1)}, u32[]{:S(2)}, u32[]{:S(2)}) collective-permute-start(bf16[512,768]{0,1:T(8,128)(2,1)} %bitcast.101), channel_id=1, source_target_pairs={{0,16},{8,24},{16,0},{24,8},{1,17},{9,25},{17,1},{25,9},{2,18},{10... | collective-permute-start | bytes 2359304 | tf_op jit(solution)/shard_map/ppermute | solution.py:301
  8.7 34.4 %collective-permute-start = (bf16[512,768]{0,1:T(8,128)(2,1)S(1)}, bf16[512,768]{0,1:T(8,128)(2,1)}, u32[]{:S(2)}, u32[]{:S(2)}) collective-permute-start(bf16[512,768]{0,1:T(8,128)(2,1)S(1)} %bitcast.102), channel_id=1, source_target_pairs={{0,16},{8,24},{16,0},{24,8},{1,17},{9,25},{17,1},{25,9},{2,18},{10... | collective-permute-start | bytes 2359304 | tf_op jit(solution)/shard_map/ppermute | solution.py:301
  173.1 115.2 %collective-permute-start.3 = (bf16[512,768]{0,1:T(8,128)(2,1)}, bf16[512,768]{0,1:T(8,128)(2,1)}, u32[]{:S(2)}, u32[]{:S(2)}) collective-permute-start(bf16[512,768]{0,1:T(8,128)(2,1)} %get-tuple-element.134), channel_id=1, source_target_pairs={{0,16},{8,24},{16,0},{24,8},{1,17},{9,25},{17,1},{25,9},{2,18},{10... | collective-permute-start | bytes 2359304 | tf_op jit(solution)/shard_map/ppermute | solution.py:301
  205.0 11.9 %collective-permute-start.5 = (bf16[1024,384]{1,0:T(8,128)(2,1)S(1)}, bf16[1024,384]{1,0:T(8,128)(2,1)S(1)}, u32[]{:S(2)}, u32[]{:S(2)}) collective-permute-start(bf16[1024,384]{1,0:T(8,128)(2,1)S(1)} %get-tuple-element.132), channel_id=1, source_target_pairs={{0,8},{8,0},{16,24},{24,16},{1,9},{9,1},{17,25},{25,17},{2,10},{10... | collective-permute-start | bytes 2359304 | tf_op jit(solution)/shard_map/ppermute | solution.py:301
  208.6 188.7 %collective-permute-start.53 = (bf16[384,3072]{1,0:T(8,128)(2,1)}, bf16[384,3072]{1,0:T(8,128)(2,1)}, u32[]{:S(2)}, u32[]{:S(2)}) collective-permute-start(bf16[384,3072]{1,0:T(8,128)(2,1)} %constant_dynamic-slice_fusion.11), channel_id=1, source_target_pairs={{0,8},{8,0},{16,24},{24,16},{1,9},{9,1},{17,25},{25,17},{2,10},{10... | collective-permute-start | bytes 7077896 | tf_op jit(solution)/shard_map/ppermute | solution.py:301
  213.0 100.0 %collective-permute-start.42 = (bf16[112,768]{1,0:T(8,128)(2,1)}, bf16[112,768]{1,0:T(8,128)(2,1)}, u32[]{:S(2)}, u32[]{:S(2)}) collective-permute-start(bf16[112,768]{1,0:T(8,128)(2,1)} %get-tuple-element.157), channel_id=1, source_target_pairs={{0,2},{1,3},{2,4},{3,5},{4,6},{5,7},{6,0},{7,1},{8,10},{9,11},{10,... | collective-permute-start | bytes 516104 | tf_op jit(solution)/shard_map/ppermute | solution.py:301
  214.6 100.0 %collective-permute-start.44 = (bf16[112,768]{1,0:T(8,128)(2,1)}, bf16[112,768]{1,0:T(8,128)(2,1)}, u32[]{:S(2)}, u32[]{:S(2)}) collective-permute-start(bf16[112,768]{1,0:T(8,128)(2,1)} %get-tuple-element.158), channel_id=1, source_target_pairs={{0,6},{1,7},{2,0},{3,1},{4,2},{5,3},{6,4},{7,5},{8,14},{9,15},{10,... | collective-permute-start | bytes 516104 | tf_op jit(solution)/shard_map/ppermute | solution.py:301
  216.8 100.0 %collective-permute-start.43 = (bf16[112,768]{1,0:T(8,128)(2,1)}, bf16[112,768]{1,0:T(8,128)(2,1)}, u32[]{:S(2)}, u32[]{:S(2)}) collective-permute-start(bf16[112,768]{1,0:T(8,128)(2,1)} %get-tuple-element.159), channel_id=1, source_target_pairs={{0,4},{1,5},{2,6},{3,7},{4,0},{5,1},{6,2},{7,3},{8,12},{9,13},{10,... | collective-permute-start | bytes 516104 | tf_op jit(solution)/shard_map/ppermute | solution.py:301
  300.7 40.7 %collective-permute-start.19 = (bf16[384,384]{1,0:T(8,128)(2,1)S(1)}, bf16[384,384]{1,0:T(8,128)(2,1)S(1)}, u32[]{:S(2)}, u32[]{:S(2)}) collective-permute-start(bf16[384,384]{1,0:T(8,128)(2,1)S(1)} %constant_dynamic-slice_fusion.27), channel_id=1, source_target_pairs={{0,1},{1,0},{2,3},{3,2},{4,5},{5,4},{6,7},{7,6},{8,9},{9,8},{10,11... | collective-permute-start | bytes 884744 | tf_op jit(solution)/shard_map/ppermute | solution.py:301
  316.9 13.2 %collective-permute-start.31 = (bf16[200,384]{1,0:T(8,128)(2,1)S(1)}, bf16[200,384]{1,0:T(8,128)(2,1)S(1)}, u32[]{:S(2)}, u32[]{:S(2)}) collective-permute-start(bf16[200,384]{1,0:T(8,128)(2,1)S(1)} %get-tuple-element.162), channel_id=1, source_target_pairs={{0,4},{1,5},{2,6},{3,7},{4,0},{5,1},{6,2},{7,3},{8,12},{9,13},{10,... | collective-permute-start | bytes 460808 | tf_op jit(solution)/shard_map/ppermute | solution.py:301
  321.7 25.1 %collective-permute-start.8 = (bf16[400,384]{1,0:T(8,128)(2,1)S(1)}, bf16[400,384]{1,0:T(8,128)(2,1)S(1)}, u32[]{:S(2)}, u32[]{:S(2)}) collective-permute-start(bf16[400,384]{1,0:T(8,128)(2,1)S(1)} %constant_dynamic-slice_fusion.32), channel_id=1, source_target_pairs={{0,16},{8,24},{16,0},{24,8},{1,17},{9,25},{17,1},{25,9},{2,18},{10... | collective-permute-start | bytes 921608 | tf_op jit(solution)/shard_map/ppermute | solution.py:301
  338.8 12.2 %collective-permute-start.48 = (bf16[56,768]{1,0:T(8,128)(2,1)S(1)}, bf16[56,768]{1,0:T(8,128)(2,1)S(1)}, u32[]{:S(2)}, u32[]{:S(2)}) collective-permute-start(bf16[56,768]{1,0:T(8,128)(2,1)S(1)} %pad_maximum_fusion.19), channel_id=1, source_target_pairs={{0,16},{8,24},{16,0},{24,8},{1,17},{9,25},{17,1},{25,9},{2,18},{10... | collective-permute-start | bytes 258056 | tf_op jit(solution)/shard_map/ppermute | solution.py:301
  341.5 11.2 %collective-permute-start.20 = (bf16[96,384]{1,0:T(8,128)(2,1)S(1)}, bf16[96,384]{1,0:T(8,128)(2,1)S(1)}, u32[]{:S(2)}, u32[]{:S(2)}) collective-permute-start(bf16[96,384]{1,0:T(8,128)(2,1)S(1)} %get-tuple-element.176), channel_id=1, source_target_pairs={{0,2},{1,3},{2,4},{3,5},{4,6},{5,7},{6,0},{7,1},{8,10},{9,11},{10,... | collective-permute-start | bytes 221192 | tf_op jit(solution)/shard_map/ppermute | solution.py:301
  350.9 12.3 %collective-permute-start.9 = (bf16[200,384]{1,0:T(8,128)(2,1)S(1)}, bf16[200,384]{1,0:T(8,128)(2,1)S(1)}, u32[]{:S(2)}, u32[]{:S(2)}) collective-permute-start(bf16[200,384]{1,0:T(8,128)(2,1)S(1)} %constant_dynamic-slice_fusion.31), channel_id=1, source_target_pairs={{0,1},{1,0},{2,3},{3,2},{4,5},{5,4},{6,7},{7,6},{8,9},{9,8},{10,11... | collective-permute-start | bytes 460808 | tf_op jit(solution)/shard_map/ppermute | solution.py:301
  353.2 25.0 %collective-permute-start.50 = (bf16[112,768]{1,0:T(8,128)(2,1)S(1)}, bf16[112,768]{1,0:T(8,128)(2,1)}, u32[]{:S(2)}, u32[]{:S(2)}) collective-permute-start(bf16[112,768]{1,0:T(8,128)(2,1)S(1)} %get-tuple-element.179), channel_id=1, source_target_pairs={{0,4},{1,5},{2,6},{3,7},{4,0},{5,1},{6,2},{7,3},{8,12},{9,13},{10,... | collective-permute-start | bytes 516104 | tf_op jit(solution)/shard_map/ppermute | solution.py:301
  373.5 21.0 %collective-permute-start.37 = (bf16[200,384]{1,0:T(8,128)(2,1)}, bf16[200,384]{1,0:T(8,128)(2,1)}, u32[]{:S(2)}, u32[]{:S(2)}) collective-permute-start(bf16[200,384]{1,0:T(8,128)(2,1)} %get-tuple-element.117), channel_id=1, source_target_pairs={{0,2},{1,3},{2,4},{3,5},{4,6},{5,7},{6,0},{7,1},{8,10},{9,11},{10,... | collective-permute-start | bytes 460808 | tf_op jit(solution)/shard_map/ppermute | solution.py:301
  391.6 51.3 %collective-permute-start.65 = (bf16[1536,768]{1,0:T(8,128)(2,1)}, bf16[1536,768]{1,0:T(8,128)(2,1)}, u32[]{:S(2)}, u32[]{:S(2)}) collective-permute-start(bf16[1536,768]{1,0:T(8,128)(2,1)} %constant_dynamic-slice_fusion.5), channel_id=1, source_target_pairs={{0,8},{8,0},{16,24},{24,16},{1,9},{9,1},{17,25},{25,17},{2,10},{10... | collective-permute-start | bytes 7077896 | tf_op jit(solution)/shard_map/ppermute | solution.py:301
  391.9 214.6 %collective-permute-start.6 = (bf16[1024,768]{0,1:T(8,128)(2,1)}, bf16[1024,768]{0,1:T(8,128)(2,1)}, u32[]{:S(2)}, u32[]{:S(2)}) collective-permute-start(bf16[1024,768]{0,1:T(8,128)(2,1)} %slice.138), channel_id=1, source_target_pairs={{0,8},{8,0},{16,24},{24,16},{1,9},{9,1},{17,25},{25,17},{2,10},{10... | collective-permute-start | bytes 4718600 | tf_op jit(solution)/shard_map/ppermute | solution.py:301
  393.0 11.2 %collective-permute-start.38 = (bf16[200,384]{1,0:T(8,128)(2,1)}, bf16[200,384]{1,0:T(8,128)(2,1)S(1)}, u32[]{:S(2)}, u32[]{:S(2)}) collective-permute-start(bf16[200,384]{1,0:T(8,128)(2,1)} %get-tuple-element.117), channel_id=1, source_target_pairs={{0,4},{1,5},{2,6},{3,7},{4,0},{5,1},{6,2},{7,3},{8,12},{9,13},{10,... | collective-permute-start | bytes 460808 | tf_op jit(solution)/shard_map/ppermute | solution.py:301
  394.5 12.2 %collective-permute-start.39 = (bf16[200,384]{1,0:T(8,128)(2,1)}, bf16[200,384]{1,0:T(8,128)(2,1)S(1)}, u32[]{:S(2)}, u32[]{:S(2)}) collective-permute-start(bf16[200,384]{1,0:T(8,128)(2,1)} %get-tuple-element.117), channel_id=1, source_target_pairs={{0,6},{1,7},{2,0},{3,1},{4,2},{5,3},{6,4},{7,5},{8,14},{9,15},{10,... | collective-permute-start | bytes 460808 | tf_op jit(solution)/shard_map/ppermute | solution.py:301
  397.3 39.0 %collective-permute-start.28 = (bf16[384,384]{1,0:T(8,128)(2,1)S(1)}, bf16[384,384]{1,0:T(8,128)(2,1)S(1)}, u32[]{:S(2)}, u32[]{:S(2)}) collective-permute-start(bf16[384,384]{1,0:T(8,128)(2,1)S(1)} %constant_dynamic-update-slice_fusion.12), channel_id=1, source_target_pairs={{0,1},{1,0},{2,3},{3,2},{4,5},{5,4},{6,7},{7,6},{8,9},{9,8},{10,11... | collective-permute-start | bytes 884744 | tf_op jit(solution)/shard_map/ppermute | solution.py:301
  404.2 33.2 %collective-permute-start.54 = (bf16[192,3072]{1,0:T(8,128)(2,1)S(1)}, bf16[192,3072]{1,0:T(8,128)(2,1)S(1)}, u32[]{:S(2)}, u32[]{:S(2)}) collective-permute-start(bf16[192,3072]{1,0:T(8,128)(2,1)S(1)} %constant_dynamic-slice_fusion.10), channel_id=1, source_target_pairs={{0,1},{1,0},{2,3},{3,2},{4,5},{5,4},{6,7},{7,6},{8,9},{9,8},{10,11... | collective-permute-start | bytes 3538952 | tf_op jit(solution)/shard_map/ppermute | solution.py:301
  406.7 29.6 %collective-permute-start.16 = (bf16[200,384]{1,0:T(8,128)(2,1)S(1)}, bf16[200,384]{1,0:T(8,128)(2,1)S(1)}, u32[]{:S(2)}, u32[]{:S(2)}) collective-permute-start(bf16[200,384]{1,0:T(8,128)(2,1)S(1)} %dynamic_update_slice.79), channel_id=1, source_target_pairs={{0,1},{1,0},{2,3},{3,2},{4,5},{5,4},{6,7},{7,6},{8,9},{9,8},{10,11... | collective-permute-start | bytes 460808 | tf_op jit(solution)/shard_map/ppermute | solution.py:301
  436.2 76.0 %collective-permute-start.40 = (bf16[1,800,384]{2,1,0:T(8,128)(2,1)S(1)}, bf16[1,800,384]{2,1,0:T(8,128)(2,1)S(1)}, u32[]{:S(2)}, u32[]{:S(2)}) collective-permute-start(bf16[1,800,384]{2,1,0:T(8,128)(2,1)S(1)} %bitcast_dynamic-update-slice_fusion), channel_id=1, source_target_pairs={{0,8},{8,0},{16,24},{24,16},{1,9},{9,1},{17,25},{25,17},{2,10},{10... | collective-permute-start | bytes 1843208 | tf_op jit(solution)/shard_map/ppermute | solution.py:301
  437.9 12.8 %collective-permute-start.55 = (bf16[48,3072]{1,0:T(8,128)(2,1)S(1)}, bf16[48,3072]{1,0:T(8,128)(2,1)S(1)}, u32[]{:S(2)}, u32[]{:S(2)}) collective-permute-start(bf16[48,3072]{1,0:T(8,128)(2,1)S(1)} %get-tuple-element.148), channel_id=1, source_target_pairs={{0,2},{1,3},{2,4},{3,5},{4,6},{5,7},{6,0},{7,1},{8,10},{9,11},{10,... | collective-permute-start | bytes 884744 | tf_op jit(solution)/shard_map/ppermute | solution.py:301
  440.1 15.5 %collective-permute-start.57 = (bf16[48,3072]{1,0:T(8,128)(2,1)S(1)}, bf16[48,3072]{1,0:T(8,128)(2,1)S(1)}, u32[]{:S(2)}, u32[]{:S(2)}) collective-permute-start(bf16[48,3072]{1,0:T(8,128)(2,1)S(1)} %get-tuple-element.149), channel_id=1, source_target_pairs={{0,6},{1,7},{2,0},{3,1},{4,2},{5,3},{6,4},{7,5},{8,14},{9,15},{10,... | collective-permute-start | bytes 884744 | tf_op jit(solution)/shard_map/ppermute | solution.py:301
  442.9 26.6 %collective-permute-start.56 = (bf16[48,3072]{1,0:T(8,128)(2,1)S(1)}, bf16[48,3072]{1,0:T(8,128)(2,1)S(1)}, u32[]{:S(2)}, u32[]{:S(2)}) collective-permute-start(bf16[48,3072]{1,0:T(8,128)(2,1)S(1)} %get-tuple-element.150), channel_id=1, source_target_pairs={{0,4},{1,5},{2,6},{3,7},{4,0},{5,1},{6,2},{7,3},{8,12},{9,13},{10,... | collective-permute-start | bytes 884744 | tf_op jit(solution)/shard_map/ppermute | solution.py:301
  450.7 19.0 %collective-permute-start.17 = (bf16[400,384]{1,0:T(8,128)(2,1)S(1)}, bf16[400,384]{1,0:T(8,128)(2,1)S(1)}, u32[]{:S(2)}, u32[]{:S(2)}) collective-permute-start(bf16[400,384]{1,0:T(8,128)(2,1)S(1)} %pad_maximum_fusion.15), channel_id=1, source_target_pairs={{0,16},{8,24},{16,0},{24,8},{1,17},{9,25},{17,1},{25,9},{2,18},{10... | collective-permute-start | bytes 921608 | tf_op jit(solution)/shard_map/ppermute | solution.py:301
  455.5 32.9 %collective-permute-start.66 = (bf16[768,768]{1,0:T(8,128)(2,1)S(1)}, bf16[768,768]{1,0:T(8,128)(2,1)S(1)}, u32[]{:S(2)}, u32[]{:S(2)}) collective-permute-start(bf16[768,768]{1,0:T(8,128)(2,1)S(1)} %constant_dynamic-slice_fusion.4), channel_id=1, source_target_pairs={{0,16},{8,24},{16,0},{24,8},{1,17},{9,25},{17,1},{25,9},{2,18},{10... | collective-permute-start | bytes 3538952 | tf_op jit(solution)/shard_map/ppermute | solution.py:301
  469.6 18.4 %collective-permute-start.58 = (bf16[24,3072]{1,0:T(8,128)(2,1)S(1)}, bf16[24,3072]{1,0:T(8,128)(2,1)S(1)}, u32[]{:S(2)}, u32[]{:S(2)}) collective-permute-start(bf16[24,3072]{1,0:T(8,128)(2,1)S(1)} %constant_dynamic-slice_fusion.6), channel_id=1, source_target_pairs={{0,16},{8,24},{16,0},{24,8},{1,17},{9,25},{17,1},{25,9},{2,18},{10... | collective-permute-start | bytes 442376 | tf_op jit(solution)/shard_map/ppermute | solution.py:301
  488.8 14.2 %collective-permute-start.67 = (bf16[384,768]{1,0:T(8,128)(2,1)S(1)}, bf16[384,768]{1,0:T(8,128)(2,1)S(1)}, u32[]{:S(2)}, u32[]{:S(2)}) collective-permute-start(bf16[384,768]{1,0:T(8,128)(2,1)S(1)} %constant_dynamic-slice_fusion.3), channel_id=1, source_target_pairs={{0,1},{1,0},{2,3},{3,2},{4,5},{5,4},{6,7},{7,6},{8,9},{9,8},{10,11... | collective-permute-start | bytes 1769480 | tf_op jit(solution)/shard_map/ppermute | solution.py:301
  493.5 30.3 %collective-permute-start.60 = (bf16[48,3072]{1,0:T(8,128)(2,1)S(1)}, bf16[48,3072]{1,0:T(8,128)(2,1)S(1)}, u32[]{:S(2)}, u32[]{:S(2)}) collective-permute-start(bf16[48,3072]{1,0:T(8,128)(2,1)S(1)} %get-tuple-element.172), channel_id=1, source_target_pairs={{0,2},{1,3},{2,4},{3,5},{4,6},{5,7},{6,0},{7,1},{8,10},{9,11},{10,... | collective-permute-start | bytes 884744 | tf_op jit(solution)/shard_map/ppermute | solution.py:301
  503.2 13.8 %collective-permute-start.68 = (bf16[96,768]{1,0:T(8,128)(2,1)S(1)}, bf16[96,768]{1,0:T(8,128)(2,1)S(1)}, u32[]{:S(2)}, u32[]{:S(2)}) collective-permute-start(bf16[96,768]{1,0:T(8,128)(2,1)S(1)} %get-tuple-element.165), channel_id=1, source_target_pairs={{0,2},{1,3},{2,4},{3,5},{4,6},{5,7},{6,0},{7,1},{8,10},{9,11},{10,... | collective-permute-start | bytes 442376 | tf_op jit(solution)/shard_map/ppermute | solution.py:301
  504.0 13.1 %collective-permute-start.70 = (bf16[96,768]{1,0:T(8,128)(2,1)S(1)}, bf16[96,768]{1,0:T(8,128)(2,1)S(1)}, u32[]{:S(2)}, u32[]{:S(2)}) collective-permute-start(bf16[96,768]{1,0:T(8,128)(2,1)S(1)} %get-tuple-element.166), channel_id=1, source_target_pairs={{0,6},{1,7},{2,0},{3,1},{4,2},{5,3},{6,4},{7,5},{8,14},{9,15},{10,... | collective-permute-start | bytes 442376 | tf_op jit(solution)/shard_map/ppermute | solution.py:301
  512.3 11.4 %collective-permute-start.69 = (bf16[96,768]{1,0:T(8,128)(2,1)S(1)}, bf16[96,768]{1,0:T(8,128)(2,1)S(1)}, u32[]{:S(2)}, u32[]{:S(2)}) collective-permute-start(bf16[96,768]{1,0:T(8,128)(2,1)S(1)} %get-tuple-element.167), channel_id=1, source_target_pairs={{0,4},{1,5},{2,6},{3,7},{4,0},{5,1},{6,2},{7,3},{8,12},{9,13},{10,... | collective-permute-start | bytes 442376 | tf_op jit(solution)/shard_map/ppermute | solution.py:301
  517.1 48.8 %collective-permute-start.52 = (bf16[448,768]{1,0:T(8,128)(2,1)S(1)}, bf16[448,768]{1,0:T(8,128)(2,1)S(1)}, u32[]{:S(2)}, u32[]{:S(2)}) collective-permute-start(bf16[448,768]{1,0:T(8,128)(2,1)S(1)} %constant_dynamic-update-slice_fusion.8), channel_id=1, source_target_pairs={{0,8},{8,0},{16,24},{24,16},{1,9},{9,1},{17,25},{25,17},{2,10},{10... | collective-permute-start | bytes 2064392 | tf_op jit(solution)/shard_map/ppermute | solution.py:301
  517.1 114.5 %collective-permute-start.29 = (bf16[1,768,384]{2,1,0:T(8,128)(2,1)}, bf16[1,768,384]{2,1,0:T(8,128)(2,1)}, u32[]{:S(2)}, u32[]{:S(2)}) collective-permute-start(bf16[1,768,384]{2,1,0:T(8,128)(2,1)} %maximum_bitcast_fusion.1), channel_id=1, source_target_pairs={{0,8},{8,0},{16,24},{24,16},{1,9},{9,1},{17,25},{25,17},{2,10},{10... | collective-permute-start | bytes 1769480 | tf_op jit(solution)/shard_map/ppermute | solution.py:301
  523.6 15.2 %collective-permute-start.61 = (bf16[48,3072]{1,0:T(8,128)(2,1)S(1)}, bf16[48,3072]{1,0:T(8,128)(2,1)S(1)}, u32[]{:S(2)}, u32[]{:S(2)}) collective-permute-start(bf16[48,3072]{1,0:T(8,128)(2,1)S(1)} %get-tuple-element.172), channel_id=1, source_target_pairs={{0,4},{1,5},{2,6},{3,7},{4,0},{5,1},{6,2},{7,3},{8,12},{9,13},{10,... | collective-permute-start | bytes 884744 | tf_op jit(solution)/shard_map/ppermute | solution.py:301
  523.8 15.1 %collective-permute-start.62 = (bf16[48,3072]{1,0:T(8,128)(2,1)S(1)}, bf16[48,3072]{1,0:T(8,128)(2,1)S(1)}, u32[]{:S(2)}, u32[]{:S(2)}) collective-permute-start(bf16[48,3072]{1,0:T(8,128)(2,1)S(1)} %get-tuple-element.172), channel_id=1, source_target_pairs={{0,6},{1,7},{2,0},{3,1},{4,2},{5,3},{6,4},{7,5},{8,14},{9,15},{10,... | collective-permute-start | bytes 884744 | tf_op jit(solution)/shard_map/ppermute | solution.py:301
  538.9 19.5 %collective-permute-start.72 = (bf16[96,768]{1,0:T(8,128)(2,1)S(1)}, bf16[96,768]{1,0:T(8,128)(2,1)S(1)}, u32[]{:S(2)}, u32[]{:S(2)}) collective-permute-start(bf16[96,768]{1,0:T(8,128)(2,1)S(1)} %get-tuple-element.109), channel_id=1, source_target_pairs={{0,4},{1,5},{2,6},{3,7},{4,0},{5,1},{6,2},{7,3},{8,12},{9,13},{10,... | collective-permute-start | bytes 442376 | tf_op jit(solution)/shard_map/ppermute | solution.py:301
  538.9 17.6 %collective-permute-start.71 = (bf16[96,768]{1,0:T(8,128)(2,1)S(1)}, bf16[96,768]{1,0:T(8,128)(2,1)S(1)}, u32[]{:S(2)}, u32[]{:S(2)}) collective-permute-start(bf16[96,768]{1,0:T(8,128)(2,1)S(1)} %get-tuple-element.109), channel_id=1, source_target_pairs={{0,2},{1,3},{2,4},{3,5},{4,6},{5,7},{6,0},{7,1},{8,10},{9,11},{10,... | collective-permute-start | bytes 442376 | tf_op jit(solution)/shard_map/ppermute | solution.py:301
  558.4 40.7 %collective-permute-start.63 = (bf16[192,3072]{1,0:T(8,128)(2,1)S(1)}, bf16[192,3072]{1,0:T(8,128)(2,1)S(1)}, u32[]{:S(2)}, u32[]{:S(2)}) collective-permute-start(bf16[192,3072]{1,0:T(8,128)(2,1)S(1)} %constant_dynamic-update-slice_fusion.4), channel_id=1, source_target_pairs={{0,1},{1,0},{2,3},{3,2},{4,5},{5,4},{6,7},{7,6},{8,9},{9,8},{10,11... | collective-permute-start | bytes 3538952 | tf_op jit(solution)/shard_map/ppermute | solution.py:301
  561.7 36.0 %collective-permute-start.74 = (bf16[384,768]{1,0:T(8,128)(2,1)S(1)}, bf16[384,768]{1,0:T(8,128)(2,1)S(1)}, u32[]{:S(2)}, u32[]{:S(2)}) collective-permute-start(bf16[384,768]{1,0:T(8,128)(2,1)S(1)} %constant_dynamic-update-slice_fusion), channel_id=1, source_target_pairs={{0,1},{1,0},{2,3},{3,2},{4,5},{5,4},{6,7},{7,6},{8,9},{9,8},{10,11... | collective-permute-start | bytes 1769480 | tf_op jit(solution)/shard_map/ppermute | solution.py:301
  565.9 68.8 %collective-permute-start.18 = (bf16[1,800,384]{2,1,0:T(8,128)(2,1)}, bf16[1,800,384]{2,1,0:T(8,128)(2,1)}, u32[]{:S(2)}, u32[]{:S(2)}) collective-permute-start(bf16[1,800,384]{2,1,0:T(8,128)(2,1)} %maximum_bitcast_fusion), channel_id=1, source_target_pairs={{0,8},{8,0},{16,24},{24,16},{1,9},{9,1},{17,25},{25,17},{2,10},{10... | collective-permute-start | bytes 1843208 | tf_op jit(solution)/shard_map/ppermute | solution.py:301
  599.0 29.2 %collective-permute-start.75 = (bf16[768,768]{1,0:T(8,128)(2,1)}, bf16[768,768]{1,0:T(8,128)(2,1)}, u32[]{:S(2)}, u32[]{:S(2)}) collective-permute-start(bf16[768,768]{1,0:T(8,128)(2,1)} %pad_maximum_fusion.8), channel_id=1, source_target_pairs={{0,16},{8,24},{16,0},{24,8},{1,17},{9,25},{17,1},{25,9},{2,18},{10... | collective-permute-start | bytes 3538952 | tf_op jit(solution)/shard_map/ppermute | solution.py:301
  601.9 43.9 %collective-permute-start.64 = (bf16[384,3072]{1,0:T(8,128)(2,1)}, bf16[384,3072]{1,0:T(8,128)(2,1)}, u32[]{:S(2)}, u32[]{:S(2)}) collective-permute-start(bf16[384,3072]{1,0:T(8,128)(2,1)} %pad_maximum_fusion.1), channel_id=1, source_target_pairs={{0,8},{8,0},{16,24},{24,16},{1,9},{9,1},{17,25},{25,17},{2,10},{10... | collective-permute-start | bytes 7077896 | tf_op jit(solution)/shard_map/ppermute | solution.py:301
  609.4 32.4 %collective-permute-start.7 = (bf16[512,768]{0,1:T(8,128)(2,1)S(1)}, bf16[512,768]{0,1:T(8,128)(2,1)S(1)}, u32[]{:S(2)}, u32[]{:S(2)}) collective-permute-start(bf16[512,768]{0,1:T(8,128)(2,1)S(1)} %get-tuple-element.130), channel_id=1, source_target_pairs={{0,16},{8,24},{16,0},{24,8},{1,17},{9,25},{17,1},{25,9},{2,18},{10... | collective-permute-start | bytes 2359304 | tf_op jit(solution)/shard_map/ppermute | solution.py:301
  631.6 22.0 %collective-permute-start.76 = (bf16[1536,768]{1,0:T(8,128)(2,1)}, bf16[1536,768]{1,0:T(8,128)(2,1)}, u32[]{:S(2)}, u32[]{:S(2)}) collective-permute-start(bf16[1536,768]{1,0:T(8,128)(2,1)} %pad_maximum_fusion.2), channel_id=1, source_target_pairs={{0,8},{8,0},{16,24},{24,16},{1,9},{9,1},{17,25},{25,17},{2,10},{10... | collective-permute-start | bytes 7077896 | tf_op jit(solution)/shard_map/ppermute | solution.py:301
  (96 other events, 1039.0 us)
